TPU v7x, 128 devices: a whole 4x4x4 slice. The times are simulated.
128 devices in a mesh: grp: 8 (over y, core), tp: 16 (over z, x).
Axes of the slice: x: 4, y: 4, z: 4, core: 2. Of those that a mesh axis runs over, the one named last changes fastest.
Arguments:
- queries: bfloat16 [1024, 4096], P('grp', 'tp'), may hold values from -6 to 6
- new_kv: bfloat16 [1024, 16, 256], P('grp', 'tp'), may hold values from -6 to 6, as said below
- kv_cache: bfloat16 [3200, 16, 16, 256], P('grp', 'tp'), may hold values from -6 to 6, as said below
- page_table: int32 [1024, 16], P('grp'), may hold values from 0 to 399, as said below
- context_lengths: int32 [1024], P('grp'), may hold values from 1 to 256, as said below
- out_weight: bfloat16 [4096, 6144], P('tp'), may hold values from -0.09375 to 0.09375
- residual_in: bfloat16 [1024, 6144], P('grp', 'tp'), may hold values from -32 to 32
- norm_gain: float32 [6144], replicated, may hold values from 0.5 to 1.5
- router_weight: bfloat16 [6144, 8], replicated, may hold values from -0.078125 to 0.078125
- routes: int32 [1024, 2], P('grp'), may hold values from 0 to 7, all different within a row; in each aligned block of 128 rows (0 to 127, 128 to 255, ...) at most 64 rows name the same one
- gate_weight: bfloat16 [8, 6144, 8192], P('grp', None, 'tp'), may hold values from -0.078125 to 0.078125
- up_weight: bfloat16 [8, 6144, 8192], P('grp', None, 'tp'), may hold values from -0.078125 to 0.078125
- down_weight: bfloat16 [8, 8192, 6144], P('grp', 'tp'), may hold values from -0.0625 to 0.0625
Outputs:
- layer_out: bfloat16 [1024, 6144], P('grp', 'tp')
Inputs may be any that keep to these rules, and one draw needn't show every extreme that they name: `context_lengths`: cached tokens of each request, its new token not counted. In every group of 128 requests one has exactly 256, and the pages they need, ceil(length / 16) each, sum to at most 400. `page_table`: entries index the pool of the request's own group. The first ceil(length / 16) entries of all requests of one group are distinct; later entries name arbitrary pages. `routes`: two different experts for each token. Among the 128 tokens of one group at most 64 name the same expert, a bound that some group reaches. `kv_cache`: copy c holds key-value head c * 8 // 16; copies of one head are equal. `new_kv`: copy c holds key-value head c * 8 // 16; copies of one head are equal.
All inputs are finite; a program needn't handle non-finite values.
Results may differ from a plain program's by a relative error of at most 0.011.
Values may be sent and summed in bfloat16 or wider, within the bound.
A program may use at most 128 MiB of HBM per device.

v0:
```python
import jax
import jax.numpy as jnp
from jax import lax
from jax.sharding import PartitionSpec as P

EPS = 1e-05


def attention_rows(queries, new_kv, kv_cache, page_table, context_lengths):
    row_count = queries.shape[0]
    head_dim = kv_cache.shape[3] // 2
    heads_dev = queries.shape[1] // head_dim
    key_span = page_table.shape[1] * kv_cache.shape[2]
    gathered = kv_cache[page_table.reshape(-1), 0].reshape(row_count, key_span, 2 * head_dim)
    query_heads = queries.reshape(row_count, heads_dev, head_dim)
    own_pair = new_kv[:, 0, :]
    score_scale = head_dim ** (-0.5)
    scores = (
        jnp.einsum(
            "rhd,rld->rhl",
            query_heads,
            gathered[:, :, :head_dim],
            preferred_element_type=jnp.float32,
        )
        * score_scale
    )
    live_mask = (jnp.arange(key_span, dtype=jnp.int32)[None, :] < context_lengths[:, None])[
        :, None, :
    ]
    scores = jnp.where(live_mask, scores, -1e30)
    own_score = (
        jnp.einsum(
            "rhd,rd->rh", query_heads, own_pair[:, :head_dim], preferred_element_type=jnp.float32
        )
        * score_scale
    )
    row_top = jnp.maximum(jnp.max(scores, axis=2), own_score)
    weights = jnp.where(live_mask, jnp.exp(scores - row_top[:, :, None]), 0.0)
    own_weight = jnp.exp(own_score - row_top)
    row_total = jnp.sum(weights, axis=2) + own_weight
    probabilities = (weights / row_total[:, :, None]).astype(jnp.bfloat16)
    own_prob = (own_weight / row_total).astype(jnp.bfloat16)
    mixed_out = jnp.einsum(
        "rhl,rld->rhd", probabilities, gathered[:, :, head_dim:], preferred_element_type=jnp.float32
    )
    mixed_out = mixed_out + own_prob.astype(jnp.float32)[:, :, None] * own_pair[
        :, None, head_dim:
    ].astype(jnp.float32)
    return mixed_out.astype(jnp.bfloat16).reshape(row_count, heads_dev * head_dim)


def route_tables(routes, logits, capacity, experts):
    row_count = routes.shape[0]
    route_hits = (routes[:, :, None] == jnp.arange(experts, dtype=jnp.int32)[None, None, :]).astype(
        jnp.int32
    )
    flat_hits = route_hits.reshape(row_count * 2, experts)
    earlier = jnp.cumsum(flat_hits, axis=0) - flat_hits
    position = jnp.sum(earlier * flat_hits, axis=1).reshape(row_count, 2)
    target = routes * capacity + position
    slot_ids = jnp.arange(experts * capacity, dtype=jnp.int32)
    hit_float = route_hits.astype(jnp.float32)
    first_logit = jnp.sum(logits * hit_float[:, 0, :], axis=1)
    second_logit = jnp.sum(logits * hit_float[:, 1, :], axis=1)
    weight_first = jax.nn.sigmoid(first_logit - second_logit)
    weight_second = jax.nn.sigmoid(second_logit - first_logit)
    placing = target[:, :, None] == slot_ids[None, None, :]
    send_matrix = jnp.transpose(jnp.any(placing, axis=1).astype(jnp.bfloat16))
    combine = weight_first[:, None] * placing[:, 0, :].astype(jnp.float32) + weight_second[
        :, None
    ] * placing[:, 1, :].astype(jnp.float32)
    return (send_matrix, combine)


def local(
    queries,
    new_kv,
    kv_cache,
    page_table,
    context_lengths,
    out_weight,
    residual_in,
    norm_gain,
    router_weight,
    routes,
    gate_weight,
    up_weight,
    down_weight,
):
    attn = attention_rows(queries, new_kv, kv_cache, page_table, context_lengths)
    partial_value = jnp.dot(attn, out_weight, preferred_element_type=jnp.float32)
    model_width = router_weight.shape[0]
    experts = router_weight.shape[1]
    capacity = routes.shape[0] // 2
    col_width = residual_in.shape[1]
    start_col = lax.axis_index("tp") * col_width
    features = lax.all_gather(residual_in, "tp", axis=1, tiled=True)
    summed = lax.psum(partial_value.astype(jnp.bfloat16), "tp").astype(jnp.float32)
    resid_full = (features.astype(jnp.float32) + summed).astype(jnp.bfloat16)
    wide_resid = resid_full.astype(jnp.float32)
    row_scale = lax.rsqrt(jnp.mean(wide_resid * wide_resid, axis=1, keepdims=True) + EPS)
    normed = (wide_resid * row_scale * norm_gain[None, :]).astype(jnp.bfloat16)
    logits = jnp.dot(normed, router_weight, preferred_element_type=jnp.float32)
    send_matrix, combine = route_tables(routes, logits, capacity, experts)
    outgoing = jnp.dot(send_matrix, normed, preferred_element_type=jnp.float32).astype(jnp.bfloat16)
    incoming = lax.all_to_all(
        outgoing.reshape(experts, capacity, model_width),
        "grp",
        split_axis=0,
        concat_axis=0,
        tiled=True,
    )
    arrived = incoming.reshape(-1, model_width)
    gate_act = jnp.dot(arrived, gate_weight[0], preferred_element_type=jnp.float32)
    up_act = jnp.dot(arrived, up_weight[0], preferred_element_type=jnp.float32)
    resid_part = lax.dynamic_slice_in_dim(resid_full, start_col, col_width, 1)
    hidden = (jax.nn.silu(gate_act) * up_act).astype(jnp.bfloat16)
    down_part = jnp.dot(hidden, down_weight[0], preferred_element_type=jnp.float32)
    sources = down_part.shape[0] // capacity
    expert_rows = lax.psum_scatter(
        down_part.astype(jnp.bfloat16), "tp", scatter_dimension=1, tiled=True
    ).astype(jnp.float32)
    returned = lax.all_to_all(
        expert_rows.reshape(sources, capacity, col_width).astype(jnp.bfloat16),
        "grp",
        split_axis=0,
        concat_axis=0,
        tiled=True,
    ).astype(jnp.float32)
    mixture = jnp.dot(combine, returned.reshape(-1, col_width), precision=lax.Precision.HIGHEST)
    return (resid_part.astype(jnp.float32) + mixture).astype(jnp.bfloat16)


def solution(mesh):
    return jax.shard_map(
        local,
        mesh=mesh,
        in_specs=(
            P("grp", "tp"),
            P("grp", "tp", None),
            P("grp", "tp", None, None),
            P("grp", None),
            P("grp"),
            P("tp", None),
            P("grp", "tp"),
            P(),
            P(),
            P("grp", None),
            P("grp", None, "tp"),
            P("grp", None, "tp"),
            P("grp", "tp", None),
        ),
        out_specs=P("grp", "tp"),
        check_vma=False,
    )
```

profile of v0, /device:TPU:1, one launch (start us, length us, event | category | flops | bytes accessed | tf_op | source)
XLA Modules:
  0.0 390.3 jit_solution(15828575418599648969)
XLA Ops:
  6.5 1.5 iota_compare_fusion.1
  8.1 0.8 copy.38
  8.9 0.1 reshape.135
  9.0 1.5 reshape.137
  10.5 19.3 %gather_fusion = bf16[2048,16,256]{2,1,0:T(8,128)(2,1)} fusion(bf16[400,1,16,256]{3,2,1,0:T(8,128)(2,1)S(1)} %copy-done, s32[2048]{0:T(1024)S(1)} %bitcast.78), kind=kCustom, calls=%fused_computation | custom fusion | bytes 33570816 | tf_op jit(solution)/shard_map/gather | solution.py:14
  29.8 5.8 %fusion.67 = (f32[128,2]{1,0:T(8,128)S(1)}, f32[128,2,256]{2,1,0:T(2,128)S(1)}) fusion(bf16[128,2,128]{2,1,0:T(2,128)(2,1)} %reshape.137, bf16[128,256,256]{2,1,0:T(8,128)(2,1)} %bitcast.81, pred[128,256]{1,0:T(8,128)(4,1)} %iota_compare_fusion.1), kind=kOutput, calls=%fused_computation.81 | convolution fusion | flops 16973568 | bytes 8750080 | tf_op jit(solution)/shard_map/rhd,rld->rhl/dot_general | solution.py:19
  35.6 0.1 copy.39
  35.6 0.7 slice_convert_fusion
  36.3 0.3 fusion.49
  36.6 0.1 copy.48
  36.7 0.1 copy.40
  36.8 0.4 fusion.51
  37.2 0.1 copy.41
  37.3 0.8 copy.42
  38.1 0.7 copy.43
  38.8 4.9 %fusion.25 = bf16[128,2,128]{2,1,0:T(2,128)(2,1)S(1)} fusion(bf16[128,256,256]{2,1,0:T(8,128)(2,1)} %bitcast.82, f32[128,2]{1,0:T(8,128)} %copy.42, f32[128,128]{1,0:T(8,128)} %get-tuple-element.9, f32[128,2]{1,0:T(8,128)} %copy.43, f32[128,2,256]{2,1,0:T(2,128)S(1)} %get-tuple-element.18, pred[128,256]{1,0:T(8,128)(4,1)} %iota_compare_fusion.1, ...), kind=kOutput, calls=%fused_computation.25 | convolution fusion | flops 17137664 | bytes 8946688 | tf_op jit(solution)/shard_map/rhl,rld->rhd/dot_general | solution.py:43
  43.8 1.7 convolution_convert_fusion.2
  45.5 0.0 all-reduce.3.cloned.1.call-update
  45.6 0.0 all-gather.2.cloned.1.call-start
  45.6 0.7 all-gather.2.cloned.1.call-update
  46.3 0.0 reduce-scatter.4.cloned.1.call-start
  46.4 0.1 copy.44
  46.5 0.1 eq.49
  46.6 0.1 eq.45
  46.8 0.6 reduce-window.6
  47.4 0.2 slice_reduce_fusion
  47.6 0.1 fusion.56
  47.7 0.1 reshape.140
  47.9 0.1 copy.46
  47.9 0.2 iota_compare_fusion
  48.1 88.1 %all-reduce.3.cloned.1.call-done = bf16[128,6144]{1,0:T(8,128)(2,1)} async-done(((bf16[128,6144]{1,0:T(8,128)(2,1)}), bf16[128,6144]{1,0:T(8,128)(2,1)}) %all-reduce.3.cloned.1.call-update) | async-done | bytes 1572880 | tf_op jit(solution)/shard_map/psum | solution.py:98
  136.2 47.1 %all-gather.2.cloned.1.call-done = bf16[128,6144]{1,0:T(8,128)(2,1)} async-done(((bf16[128,384]{1,0:T(8,128)(2,1)}), bf16[128,6144]{1,0:T(8,128)(2,1)}) %all-gather.2.cloned.1.call-update) | async-done | bytes 1572880 | tf_op jit(solution)/shard_map/all_gather | solution.py:97
  183.3 2.5 fusion.9
  185.9 1.9 convolution_convert_fusion.1
  187.8 0.0 slice-start.1
  187.8 78.4 %all_to_all.10 = bf16[8,64,6144]{2,1,0:T(8,128)(2,1)S(1)} all-to-all(bf16[8,64,6144]{2,1,0:T(8,128)(2,1)S(1)} %bitcast.79), channel_id=1, replica_groups=mesh['grp'=8,'tp'=16] {'grp'}, dimensions={0} | all-to-all | bytes 12582912 | tf_op jit(solution)/shard_map/all_to_all | solution.py:106
  266.2 3.4 fusion.7
  269.7 0.0 slice-start.5
  269.7 3.5 fusion.15
  273.2 5.3 %convolution_convert_fusion = bf16[512,6144]{1,0:T(8,128)(2,1)} fusion(bf16[512,512]{1,0:T(8,128)(2,1)S(1)} %fusion.15, bf16[1,512,6144]{2,1,0:T(8,128)(2,1)S(1)} %bitcast.94), kind=kOutput, calls=%fused_computation.1 | convolution fusion | flops 3224371200 | bytes 13107200 | tf_op jit(solution)/shard_map/dot_general | solution.py:118
  278.5 8.6 %copy.49 = bf16[512,6144]{0,1:T(8,128)(2,1)} copy(bf16[512,6144]{1,0:T(8,128)(2,1)} %convolution_convert_fusion) | data formatting | bytes 12582912
  287.2 0.0 reduce-scatter.4.cloned.1.call-update
  287.2 78.2 %reduce-scatter.4.cloned.1.call-done = bf16[384,512]{1,0:T(8,128)(2,1)} async-done(((bf16[6144,512]{1,0:T(8,128)(2,1)}), bf16[384,512]{1,0:T(8,128)(2,1)}) %reduce-scatter.4.cloned.1.call-update) | async-done | bytes 393232
  365.4 1.9 copy.50
  367.4 6.1 %all-to-all-start.1 = ((bf16[8,64,384]{2,1,0:T(8,128)(2,1)}), bf16[8,64,384]{2,1,0:T(8,128)(2,1)}, u32[]{:S(2)}, u32[]{:S(2)}) async-start(bf16[8,64,384]{2,1,0:T(8,128)(2,1)} %bitcast.85), calls=%async_computation.1 | async-start | bytes 786432 | tf_op jit(solution)/shard_map/all_to_all | solution.py:123
  373.4 2.0 fusion.61
  375.4 6.2 %all-to-all-done.1 = bf16[8,64,384]{2,1,0:T(8,128)(2,1)} async-done(((bf16[8,64,384]{2,1,0:T(8,128)(2,1)}), bf16[8,64,384]{2,1,0:T(8,128)(2,1)}, u32[]{:S(2)}, u32[]{:S(2)}) %all-to-all-start.1) | async-done | bytes 393248 | tf_op jit(solution)/shard_map/all_to_all | solution.py:123
  381.6 2.2 fusion.18
  (44 shorter events, 0.2 us)
Async XLA Ops:
  6.5 3.9 %copy-start = (bf16[400,1,16,256]{3,2,1,0:T(8,128)(2,1)S(1)}, bf16[400,1,16,256]{3,2,1,0:T(8,128)(2,1)}, u32[]{:S(2)}) copy-start(bf16[400,1,16,256]{3,2,1,0:T(8,128)(2,1)} %param.15) | copy-start | bytes 9830404
  6.5 129.7 %all-reduce.3.cloned.1.call-start = ((), (), s32[]{:S(2)}) async-start(), calls=%async_computation.4 | async-start | bytes 3145728 | tf_op jit(solution)/shard_map/psum | solution.py:98
  29.8 5.9 %copy-start.5 = (bf16[128,1,256]{2,0,1:T(8,128)(2,1)S(1)}, bf16[128,1,256]{2,0,1:T(8,128)(2,1)}, u32[]{:S(2)}) copy-start(bf16[128,1,256]{2,0,1:T(8,128)(2,1)} %param.14) | copy-start | bytes 196612
  29.8 6.6 %copy-start.6 = (bf16[128,2,128]{2,1,0:T(2,128)(2,1)S(1)}, bf16[128,2,128]{2,1,0:T(2,128)(2,1)}, u32[]{:S(2)}) copy-start(bf16[128,2,128]{2,1,0:T(2,128)(2,1)} %reshape.137) | copy-start | bytes 196612
  29.8 7.0 %copy-start.4 = (pred[128,256]{1,0:T(8,128)(4,1)S(1)}, pred[128,256]{1,0:T(8,128)(4,1)}, u32[]{:S(2)}) copy-start(pred[128,256]{1,0:T(8,128)(4,1)} %iota_compare_fusion.1) | copy-start | bytes 98308
  38.8 5.0 %copy-start.3 = (bf16[256,6144]{1,0:T(8,128)(2,1)S(1)}, bf16[256,6144]{1,0:T(8,128)(2,1)}, u32[]{:S(2)}) copy-start(bf16[256,6144]{1,0:T(8,128)(2,1)} %param.18) | copy-start | bytes 9437188
  43.8 2.6 copy-start.8
  45.5 140.3 %copy-start.7 = (f32[6144]{0:T(1024)S(1)}, f32[6144]{0:T(1024)}, u32[]{:S(2)}) copy-start(f32[6144]{0:T(1024)} %param.20) | copy-start | bytes 73732
  45.6 137.7 %all-gather.2.cloned.1.call-start = ((), (), s32[]{:S(2)}) async-start(), calls=%async_computation.3 | async-start | bytes 1671168 | tf_op jit(solution)/shard_map/all_gather | solution.py:97
  46.3 319.1 %reduce-scatter.4.cloned.1.call-start = ((), (), s32[]{:S(2)}) async-start(), calls=%async_computation.5 | async-start | bytes 6684672
  185.8 2.0 copy-start.2
  185.9 80.3 %slice-start = ((s8[6291456]{0:T(1024)(128)(4,1)}), s8[4194304]{0:T(1024)(128)(4,1)S(1)}, s32[]{:S(2)}) async-start(s8[6291456]{0:T(1024)(128)(4,1)} %bitcast.89), calls=%async_computation.6 | async-start | bytes 8388608
  187.8 78.4 %slice-start.1 = ((s8[6291456]{0:T(1024)(128)(4,1)}), s8[2097152]{0:T(1024)(128)(4,1)S(1)}, s32[]{:S(2)}) async-start(s8[6291456]{0:T(1024)(128)(4,1)} %bitcast.89), calls=%async_computation.7 | async-start | bytes 4194304
  187.8 81.8 %slice-start.2 = ((s8[6291456]{0:T(1024)(128)(4,1)}), s8[4194304]{0:T(1024)(128)(4,1)S(1)}, s32[]{:S(2)}) async-start(s8[6291456]{0:T(1024)(128)(4,1)} %bitcast.91), calls=%async_computation.8 | async-start | bytes 8388608
  266.2 3.4 slice-start.3
  266.2 6.9 %slice-start.4 = ((s8[6291456]{0:T(1024)(128)(4,1)}), s8[4194304]{0:T(1024)(128)(4,1)S(1)}, s32[]{:S(2)}) async-start(s8[6291456]{0:T(1024)(128)(4,1)} %bitcast.93), calls=%async_computation.10 | async-start | bytes 8388608
  269.7 3.5 slice-start.5
  287.2 86.3 %copy-start.9 = (bf16[6144,8]{0,1:T(8,128)(2,1)S(1)}, bf16[6144,8]{0,1:T(8,128)(2,1)}, u32[]{:S(2)}) copy-start(bf16[6144,8]{0,1:T(8,128)(2,1)} %param.21) | copy-start | bytes 294916
  287.2 96.6 %copy-start.1 = (bf16[400,1,16,256]{3,2,1,0:T(8,128)(2,1)S(1)}, bf16[400,1,16,256]{3,2,1,0:T(8,128)(2,1)}, u32[]{:S(2)}) copy-start(bf16[400,1,16,256]{3,2,1,0:T(8,128)(2,1)} %param.15) | copy-start | bytes 9830404
  367.4 14.2 %all-to-all-start.1 = ((bf16[8,64,384]{2,1,0:T(8,128)(2,1)}), bf16[8,64,384]{2,1,0:T(8,128)(2,1)}, u32[]{:S(2)}, u32[]{:S(2)}) async-start(bf16[8,64,384]{2,1,0:T(8,128)(2,1)} %bitcast.85), calls=%async_computation.1 | async-start | bytes 786432 | tf_op jit(solution)/shard_map/all_to_all | solution.py:123
Sparse Core Ops, SparseCore 0:
  45.7 90.4 all-reduce.2
  138.3 44.9 all-gather.1
  287.3 78.0 reduce-scatter.3
where the time goes:
time: 391 us; the launch traced here: 390 us
  waiting for transfers between devices  220 us (56%)
  blocking collectives  78.4 us (20%)
  local copies, waits for them, and re-layouts  34.9 us (9%)
  matrix products  31 us (8%)
  between operations  13.4 us (3%)
  other arithmetic  6.14 us (2%)
  starting transfers between devices  6.13 us (2%)
    psum x1, waiting for transfers between devices, local(): lax.psum(partial_value.astype(jnp.bfloat16), 'tp').astype(jnp.float32)  88.1 us
    unnamed x4, waiting for transfers between devices  78.9 us
    all_to_all x1, blocking collectives, local(): lax.all_to_all(outgoing.reshape(experts, capacity, model_width), 'grp', s...  78.4 us
    all_gather x1, waiting for transfers between devices, local(): features = lax.all_gather(residual_in, 'tp', axis=1, tiled=True)  47.1 us
    gather x1, local copies, waits for them, and re-layouts, attention_rows(): kv_cache[page_table.reshape(-1), 0]  19.3 us
    unnamed x36, local copies, waits for them, and re-layouts  11.6 us
  transfers between devices with their start and end apart: 4, of which 4 were waited for; matrix products, arithmetic and copies ran while one was open for 1% of the time, Pallas kernels for 0%

commit v1 on v0

v1 whole, which is shorter than its diff:
```python
import jax
import jax.numpy as jnp
from jax import lax
from jax.experimental import pallas as pl
from jax.experimental.pallas import tpu as pltpu
from jax.sharding import PartitionSpec as P

F32 = jnp.float32
BF16 = jnp.bfloat16
NEG = -1e30


def attn_kernel(q_ref, own_ref, pt_ref, len_ref, kv_hbm, w_hbm, out_ref, kv, w, cnt, sc, kvsem, wsem):
    pool = kv.shape[0]
    pages = pool // 16
    parts = kvsem.shape[0]
    step = pool // parts
    kv_copies = [
        pltpu.make_async_copy(kv_hbm.at[pl.ds(i * step, step)], kv.at[pl.ds(i * step, step)], kvsem.at[i])
        for i in range(parts)
    ]
    for c in kv_copies:
        c.start()
    wcopy = pltpu.make_async_copy(w_hbm, w, wsem)
    wcopy.start()
    pt = pt_ref[...]
    lens = len_ref[...]
    page_ids = lax.broadcasted_iota(jnp.int32, (pages, 128), 0)
    live = jnp.zeros((pages, 128), jnp.int32)
    for j in range(16):
        here = jnp.clip(lens - 16 * j, 0, 16)
        live = live + jnp.where(page_ids == pt[j : j + 1, :], here, 0)
    cnt[...] = live.astype(F32).astype(BF16)
    q = q_ref[...]
    q2 = jnp.concatenate([q[:, :128], q[:, 128:]], axis=0)
    nt = (((1,), (1,)), ((), ()))
    tn = (((0,), (0,)), ((), ()))
    tok = lax.broadcasted_iota(jnp.int32, (256, 128), 0)
    offs = (tok & 15).astype(F32)
    tok16 = lax.broadcasted_iota(jnp.int32, (256, 16), 0) >> 4
    spread = (tok16 == lax.broadcasted_iota(jnp.int32, (256, 16), 1)).astype(F32).astype(BF16)

    own = own_ref[...]
    s_own = lax.dot_general(own[:, :128], q2, nt, preferred_element_type=F32)
    row = lax.broadcasted_iota(jnp.int32, (128, 128), 0)
    col = lax.broadcasted_iota(jnp.int32, (128, 128), 1)
    eye = row == col
    eye2 = jnp.concatenate([eye.astype(F32), eye.astype(F32)], axis=1) > 0.5
    s_own = jnp.where(eye2, s_own, NEG)
    top = jnp.max(s_own.reshape(16, 8, 256), axis=0)

    per = step // 256

    def pass1(c, top):
        k = kv[pl.ds(pl.multiple_of(c * 256, 256), 256), :128]
        s = lax.dot_general(k, q2, nt, preferred_element_type=F32)
        cn = cnt[pl.ds(pl.multiple_of(c * 16, 16), 16), :]
        m = offs < jnp.dot(spread, cn, preferred_element_type=F32)
        s = jnp.concatenate([jnp.where(m, s[:, :128], NEG), jnp.where(m, s[:, 128:], NEG)], axis=1)
        sc[c] = s
        return jnp.maximum(top, jnp.max(s.reshape(32, 8, 256), axis=0))

    for i in range(parts):
        kv_copies[i].wait()
        top = lax.fori_loop(i * per, (i + 1) * per, pass1, top)
    top = jnp.max(top, axis=0, keepdims=True)
    scale = 128.0 ** -0.5

    p_own = jnp.exp((s_own - top) * scale)
    tot = jnp.sum(p_own.reshape(16, 8, 256), axis=0)
    own_v = jnp.transpose(own_ref[:, 128:].astype(F32))
    acc = jnp.concatenate([own_v, own_v], axis=1) * jnp.sum(p_own, axis=0, keepdims=True)

    def pass2(c, carry):
        tot, acc = carry
        p = jnp.exp((sc[c] - top) * scale)
        tot = tot + jnp.sum(p.reshape(32, 8, 256), axis=0)
        v = kv[pl.ds(pl.multiple_of(c * 256, 256), 256), 128:]
        acc = acc + lax.dot_general(v, p.astype(BF16), tn, preferred_element_type=F32)
        return tot, acc

    tot, acc = lax.fori_loop(0, pool // 256, pass2, (tot, acc))
    tot = jnp.sum(tot, axis=0, keepdims=True)
    att = acc / tot
    attn = jnp.concatenate([jnp.transpose(att[:, :128]), jnp.transpose(att[:, 128:])], axis=1).astype(BF16)
    wcopy.wait()
    cw = out_ref.shape[2]

    def proj(t, _):
        out_ref[t] = jnp.dot(
            attn, w[:, pl.ds(pl.multiple_of(t * cw, 128), cw)], preferred_element_type=F32
        ).astype(BF16)
        return 0

    lax.fori_loop(0, out_ref.shape[0], proj, 0)


def attention_partials(queries, new_kv, kv_cache, page_table, context_lengths, out_weight):
    pool = kv_cache.shape[0] * kv_cache.shape[2]
    vm = pl.BlockSpec(memory_space=pltpu.VMEM)
    hb = pl.BlockSpec(memory_space=pl.ANY)
    return pl.pallas_call(
        attn_kernel,
        out_shape=jax.ShapeDtypeStruct((16, 128, 384), BF16),
        in_specs=[vm, vm, vm, vm, hb, hb],
        out_specs=vm,
        scratch_shapes=[
            pltpu.VMEM((pool, 256), BF16),
            pltpu.VMEM(out_weight.shape, BF16),
            pltpu.VMEM((pool // 16, 128), BF16),
            pltpu.VMEM((pool // 256, 256, 256), F32),
            pltpu.SemaphoreType.DMA((5,)),
            pltpu.SemaphoreType.DMA,
        ],
        compiler_params=pltpu.CompilerParams(vmem_limit_bytes=40 * 1024 * 1024),
        cost_estimate=pl.CostEstimate(flops=1 << 30, bytes_accessed=8 << 20, transcendentals=1 << 21),
        name="attention",
    )(
        queries,
        new_kv.reshape(128, 256),
        page_table.T,
        context_lengths.reshape(1, 128),
        kv_cache.reshape(pool, 256),
        out_weight,
    )


MESH = pl.DeviceIdType.MESH
NT = (((1,), (1,)), ((), ()))
CW = 384
FW = 512
OFFS_OUT = (0, 3, 1, 2)
OFFS_IN = (2, 1, 3, 0)


def route_maps(routes):
    lane = lax.broadcasted_iota(jnp.int32, (128, 128), 1)
    sub = lax.broadcasted_iota(jnp.int32, (128, 128), 0)
    hit0 = (lane == routes[:, 0:1]).astype(F32)
    hit1 = (lane == routes[:, 1:2]).astype(F32)
    hit = hit0 + hit1
    hit_t = jnp.transpose(hit)
    rank = jnp.dot((lane < sub).astype(F32).astype(BF16), hit.astype(BF16), preferred_element_type=F32)
    rank_t = jnp.dot(hit_t.astype(BF16), (sub < lane).astype(F32).astype(BF16), preferred_element_type=F32)
    spot_t = jnp.where(hit_t > 0.5, rank_t, -1.0)
    slot = lax.broadcasted_iota(jnp.int32, (64, 128), 0).astype(F32)
    place = jnp.concatenate([(slot == spot_t[e : e + 1, :]).astype(F32) for e in range(8)], axis=0)
    wide = lax.broadcasted_iota(jnp.int32, (128, 512), 1)

    def back(h, col):
        at = col * 64 + jnp.sum(h * rank, axis=1, keepdims=True).astype(jnp.int32)
        return (wide == at).astype(F32).astype(BF16)

    return place.astype(BF16), back(hit0, routes[:, 0:1]), back(hit1, routes[:, 1:2])


def layer_kernel(
    part_ref, res_ref, gain_ref, router_ref, routes_ref, wg_hbm, wu_hbm, wd_hbm,
    out_ref,
    wg, wu, wd, xg, acc, ssq, hid, p2, rb1, y1, rc1, rb2, y2, rc2,
    rs, xs, ds, fin, ret, stat_out, stat_in, place, back,
    wsem, a1s, a1r, ags, agr, a2s, a2r, ds_s, ds_r, rt_s, rt_r, st_s, st_r,
):
    g = lax.axis_index("grp")
    t = lax.axis_index("tp")
    gy, gc = g // 2, lax.rem(g, 2)
    tz, tx = t // 4, lax.rem(t, 4)
    me = ((tx, tz), (tz, tx))

    def tid(h, c1, c2):
        return c2 * 4 + c1 if h == 0 else c1 * 4 + c2

    def m4(v):
        return lax.rem(v + 4, 4)

    barrier = pltpu.get_barrier_semaphore()

    def greet_t(k, c):
        pl.semaphore_signal(barrier, inc=1, device_id=(g, lax.rem(t + k, 16)), device_id_type=MESH)
        return c

    def greet_g(k, c):
        pl.semaphore_signal(barrier, inc=1, device_id=(lax.rem(g + k, 8), t), device_id_type=MESH)
        return c

    lax.fori_loop(1, 16, greet_t, 0)
    lax.fori_loop(1, 8, greet_g, 0)

    wcopies = [
        pltpu.make_async_copy(src.at[0], dst, wsem.at[i])
        for i, (src, dst) in enumerate(((wg_hbm, wg), (wu_hbm, wu), (wd_hbm, wd)))
    ]
    for c in wcopies:
        c.start()

    pl_m, b0, b1 = route_maps(routes_ref[...])
    place[...] = pl_m
    back[0] = b0
    back[1] = b1

    pl.semaphore_wait(barrier, 22)

    def rcopy(src, dst, ss, rr, dev):
        return pltpu.make_async_remote_copy(
            src_ref=src, dst_ref=dst, send_sem=ss, recv_sem=rr, device_id=dev, device_id_type=MESH
        )

    def reduce_scatter(rows, src, rb, y, rc, ss, rr, produce, finish):
        def q_rows(h, q):
            return pl.ds((2 * h + q) * rows, rows)

        def nbr(h, axis, d):
            c = list(me[h])
            c[axis] = m4(c[axis] + d)
            return (g, tid(h, c[0], c[1]))

        def blk(h, i, d2):
            return tid(h, m4(me[h][0] + OFFS_IN[i]), m4(me[h][1] + d2))

        def msg1(h, i, k, from_buf=None):
            d2, q, d = ((2, 0, 1), (2, 1, -1), (1, 1, 1), (-1, 0, -1), (1, 0, 1), (-1, 1, -1))[k]
            s = src.at[blk(h, i, d2), q_rows(h, q)] if from_buf is None else rb.at[h, i, from_buf]
            n = h * 24 + i * 6 + k
            return rcopy(s, rb.at[h, i, k], ss.at[n], rr.at[n], nbr(h, 1, d))

        def msg2(h, k, i, from_buf=None):
            q, d = ((0, 1), (1, -1), (1, 1), (0, -1), (0, 1), (1, -1))[k]
            s = y.at[h, i, pl.ds(q * rows, rows)] if from_buf is None else rc.at[h, from_buf]
            n = 48 + h * 6 + k
            return rcopy(s, rc.at[h, k], ss.at[n], rr.at[n], nbr(h, 0, d))

        sent = []

        def go(m):
            m.start()
            sent.append(m)

        def stage_g(i):
            produce(i, blk, 0)
            for h in (0, 1):
                go(msg1(h, i, 0))
                go(msg1(h, i, 1))
            produce(i, blk, 1)
            for h in (0, 1):
                go(msg1(h, i, 2))
                go(msg1(h, i, 3))

        def stage_h(i):
            for h in (0, 1):
                msg1(h, i, 0).wait_recv()
                rb[h, i, 0] = (
                    rb[h, i, 0].astype(F32) + src[blk(h, i, 1), q_rows(h, 0)].astype(F32)
                ).astype(BF16)
                go(msg1(h, i, 4, 0))
                msg1(h, i, 1).wait_recv()
                rb[h, i, 1] = (
                    rb[h, i, 1].astype(F32) + src[blk(h, i, -1), q_rows(h, 1)].astype(F32)
                ).astype(BF16)
                go(msg1(h, i, 5, 1))

        def stage_j(i):
            produce(i, blk, 2)
            for h in (0, 1):
                for q, (k1, k2) in ((0, (3, 4)), (1, (2, 5))):
                    msg1(h, i, k1).wait_recv()
                    msg1(h, i, k2).wait_recv()
                    y[h, i, pl.ds(q * rows, rows)] = (
                        src[blk(h, i, 0), q_rows(h, q)].astype(F32)
                        + rb[h, i, k1].astype(F32)
                        + rb[h, i, k2].astype(F32)
                    ).astype(BF16)
                    if i == 0:
                        go(msg2(h, q, 0))
                if i == 1:
                    go(msg2(h, 2, 1))
                    msg2(h, 0, 1).wait_recv()
                    rc[h, 0] = (rc[h, 0].astype(F32) + y[h, 1, pl.ds(0, rows)].astype(F32)).astype(BF16)
                    go(msg2(h, 4, 1, 0))
                if i == 2:
                    go(msg2(h, 3, 2))
                    msg2(h, 1, 2).wait_recv()
                    rc[h, 1] = (rc[h, 1].astype(F32) + y[h, 2, pl.ds(rows, rows)].astype(F32)).astype(BF16)
                    go(msg2(h, 5, 2, 1))

        stage_g(0)
        stage_g(1)
        stage_h(0)
        stage_j(0)
        stage_g(2)
        stage_h(1)
        stage_j(1)
        stage_g(3)
        stage_h(2)
        stage_j(2)
        stage_h(3)
        stage_j(3)
        for h in (0, 1):
            for q, (k1, k2) in ((0, (3, 4)), (1, (2, 5))):
                msg2(h, k1, 3).wait_recv()
                msg2(h, k2, 3).wait_recv()
                finish(
                    h,
                    q,
                    y[h, 3, pl.ds(q * rows, rows)].astype(F32)
                    + rc[h, k1].astype(F32)
                    + rc[h, k2].astype(F32),
                )
        return sent

    gain_row = gain_ref[pl.ds(t, 1), :]

    def finish1(h, q, v):
        at = pl.ds((2 * h + q) * 32, 32)
        r = (res_ref[at, :].astype(F32) + v).astype(BF16)
        rs[at, :] = r
        xs[at, :] = (r.astype(F32) * gain_row).astype(BF16)

    sent1 = reduce_scatter(32, part_ref, rb1, y1, rc1, a1s, a1r, lambda i, blk, s: None, finish1)

    x = xs[...]
    ds[...] = jnp.dot(place[...], x, preferred_element_type=F32).astype(BF16).reshape(8, 64, CW)

    def seat(src_y, src_c, dst_y):
        r = m4(src_y - dst_y)
        p = lax.rem(r, 2) * 2 + r // 2
        return pl.multiple_of(p * 128 + src_c * 64, 64), p * 2 + src_c

    own_row, own_slot = seat(gy, gc, gy)
    xg[t, pl.ds(own_row, 64), :] = ds[g]

    def deal(k):
        e = lax.rem(g + k, 8)
        row, slot = seat(gy, gc, e // 2)
        return rcopy(ds.at[e], xg.at[t, pl.ds(row, 64)], ds_s.at[k], ds_r.at[slot], (e, t))

    def deal_start(k, c):
        deal(k).start()
        return c

    lax.fori_loop(1, 8, deal_start, 0)

    def dealt(slot):
        at = xg.at[t, pl.ds(pl.multiple_of(slot * 64, 64), 64)]
        return rcopy(at, at, ds_s.at[0], ds_r.at[slot], (g, t))

    lane8 = lax.broadcasted_iota(jnp.int32, (128, 8), 1)
    sign = (lane8 == routes_ref[:, 0:1]).astype(F32) - (lane8 == routes_ref[:, 1:2]).astype(F32)
    logit = jnp.dot(x, router_ref[t], preferred_element_type=F32)
    diff = jnp.sum(logit * sign, axis=1, keepdims=True)
    r32 = rs[...].astype(F32)
    sq = jnp.sum(r32 * r32, axis=1, keepdims=True)
    lane = lax.broadcasted_iota(jnp.int32, (128, 128), 1)
    tile = jnp.where(lane == 0, diff, jnp.where(lane == 1, sq, 0.0))
    tile = jnp.transpose(tile)[:8, :]
    stat_out[...] = tile
    stat_in[0] = tile

    def stat(k):
        return rcopy(stat_out, stat_in.at[k], st_s.at[k], st_r.at[k], (g, lax.rem(t + k, 16)))

    def stat_start(k, c):
        stat(k).start()
        return c

    lax.fori_loop(1, 16, stat_start, 0)

    ag_sent = []

    def ag(h, phase, i, k, b):
        q, d = ((0, 1), (1, 1), (0, -1), (1, -1), (0, 1), (1, -1))[k]
        c = list(me[h])
        c[phase] = m4(c[phase] + d)
        ref = xg.at[b, pl.ds((2 * h + q) * 128, 128)]
        n = h * 30 + phase * 6 + i * 6 + k
        return rcopy(ref, ref, ags.at[n], agr.at[n], (g, tid(h, c[0], c[1])))

    def send(*a):
        m = ag(*a)
        m.start()
        ag_sent.append(m)

    def ab(h, o1, o2):
        return tid(h, m4(me[h][0] + o1), m4(me[h][1] + o2))

    def wait(h, phase, i, k, b):
        ag(h, phase, i, k, b).wait_recv()

    def spread(h, i, q):
        b = ab(h, OFFS_OUT[i], 0)
        send(h, 1, i, q, b)
        send(h, 1, i, 2 + q, b)

    def own_quarter(h, q):
        p = 2 * h + q
        for c in (0, 1):
            slot = p * 2 + c
            if p == 0:

                @pl.when(gc != c)
                def _():
                    dealt(slot).wait_recv()

            else:
                dealt(slot).wait_recv()
        send(h, 0, 0, q, t)
        send(h, 0, 0, 2 + q, t)
        spread(h, 0, q)

    def stage_p(i, h):
        if i == 1:
            b = ab(h, -1, 0)
            wait(h, 0, 0, 0, b)
            send(h, 0, 0, 4, b)
            spread(h, i, 0)
            wait(h, 0, 0, 1, b)
            spread(h, i, 1)
        elif i == 2:
            b = ab(h, 1, 0)
            wait(h, 0, 0, 3, b)
            send(h, 0, 0, 5, b)
            spread(h, i, 1)
            wait(h, 0, 0, 2, b)
            spread(h, i, 0)
        elif i == 3:
            b = ab(h, 2, 0)
            wait(h, 0, 0, 4, b)
            spread(h, i, 0)
            wait(h, 0, 0, 5, b)
            spread(h, i, 1)

    def stage_f(i, h):
        b = ab(h, OFFS_OUT[i], -1)
        wait(h, 1, i, 0, b)
        send(h, 1, i, 4, b)
        b = ab(h, OFFS_OUT[i], 1)
        wait(h, 1, i, 3, b)
        send(h, 1, i, 5, b)

    def stage_w1(i, h):
        wait(h, 1, i, 1, ab(h, OFFS_OUT[i], -1))
        wait(h, 1, i, 2, ab(h, OFFS_OUT[i], 1))

    def stage_w2(i, h):
        b = ab(h, OFFS_OUT[i], 2)
        wait(h, 1, i, 4, b)
        wait(h, 1, i, 5, b)

    def eat(o1, lo, hi):
        def body(n, c):
            h = lax.rem(n, 2)
            j = n // 2
            o2 = jnp.where(j == 0, 0, jnp.where(j == 1, 3, j - 1))
            c1 = m4(jnp.where(h == 0, tx, tz) + o1)
            c2 = m4(jnp.where(h == 0, tz, tx) + o2)
            b = jnp.where(h == 0, c2 * 4 + c1, c1 * 4 + c2)
            xb = xg[b, pl.ds(pl.multiple_of(h * 256, 256), 256), :]
            wat = pl.ds(pl.multiple_of(b * CW, CW), CW)
            acc[h, 0] += jnp.dot(xb, wg[wat, :], preferred_element_type=F32)
            acc[h, 1] += jnp.dot(xb, wu[wat, :], preferred_element_type=F32)
            v = xb.astype(F32) / gain_ref[pl.ds(b, 1), :]
            v = v * v
            ssq[h] += v[:, :128] + v[:, 128:256] + v[:, 256:]
            return c

        lax.fori_loop(lo * 2, hi * 2, body, 0)

    own_quarter(0, 0)
    acc[...] = jnp.zeros_like(acc)
    ssq[...] = jnp.zeros_like(ssq)
    own_quarter(1, 0)
    own_quarter(1, 1)
    own_quarter(0, 1)
    for h in (0, 1):
        stage_p(1, h)
    for h in (0, 1):
        stage_p(2, h)
    for h in (0, 1):
        stage_f(0, h)
    for h in (0, 1):
        stage_p(3, h)
    for h in (0, 1):
        stage_f(1, h)
    wcopies[0].wait()
    wcopies[1].wait()
    for i in (0, 1, 2, 3):
        for h in (0, 1):
            stage_w1(i, h)
        if i == 3:
            eat(OFFS_OUT[i], 0, 3)
        for h in (0, 1):
            stage_w2(i, h)
        if i < 2:
            for h in (0, 1):
                stage_f(i + 2, h)
        if i == 3:
            eat(OFFS_OUT[i], 3, 4)
        else:
            eat(OFFS_OUT[i], 0, 4)

    for h in (0, 1):
        total = jnp.sum(ssq[h], axis=1, keepdims=True)
        sc = lax.rsqrt(total / (16.0 * CW) + 1e-5)
        gate = acc[h, 0] * sc
        up = acc[h, 1] * sc
        hid[h] = (gate / (1.0 + jnp.exp(-gate)) * up).astype(BF16)
    wcopies[2].wait()

    def produce(i, blk, stage):
        todo = ((2,), (1, -1), (0,))[stage]
        for h in (0, 1):
            hv = hid[h]
            for d2 in todo:
                b = blk(h, i, d2)
                p2[b, h * 256 : (h + 1) * 256, :] = jnp.dot(
                    hv, wd[:, pl.ds(pl.multiple_of(b * CW, 128), CW)], preferred_element_type=F32
                ).astype(BF16)

    def back_copy(slot):
        p = slot // 2
        r = lax.rem(p, 2) * 2 + p // 2
        dst = lax.rem(gy + r, 4) * 2 + lax.rem(slot, 2)
        return rcopy(
            fin.at[pl.ds(pl.multiple_of(slot * 64, 64), 64)],
            ret.at[pl.ds(pl.multiple_of(g * 64, 64), 64)],
            rt_s.at[slot],
            rt_r.at[g],
            (dst, t),
        )

    def finish2(h, q, v):
        p = 2 * h + q
        fin[p * 128 : (p + 1) * 128, :] = v.astype(BF16)
        for c in (0, 1):
            slot = p * 2 + c
            if p == 0:

                @pl.when(gc != c)
                def _():
                    back_copy(slot).start()

                @pl.when(gc == c)
                def _():
                    ret[pl.ds(pl.multiple_of(g * 64, 64), 64), :] = fin[slot * 64 : slot * 64 + 64, :]

            else:
                back_copy(slot).start()

    sent2 = reduce_scatter(128, p2, rb2, y2, rc2, a2s, a2r, produce, finish2)

    def stat_wait(k, c):
        stat(k).wait_recv()
        return c

    lax.fori_loop(1, 16, stat_wait, 0)
    sums = jnp.sum(stat_in[...], axis=0)
    diff_all = sums[0:1, :] * lax.rsqrt(sums[1:2, :] / (16.0 * CW) + 1e-5)
    tile = jnp.transpose(jnp.broadcast_to(diff_all, (128, 128)))
    dcol = tile[:, 0:1]
    wa = 1.0 / (1.0 + jnp.exp(-dcol))
    wb = 1.0 / (1.0 + jnp.exp(dcol))

    def ret_wait(k, c):
        e = lax.rem(g + k, 8)
        at = ret.at[pl.ds(pl.multiple_of(e * 64, 64), 64)]
        rcopy(at, at, rt_s.at[0], rt_r.at[e], (g, t)).wait_recv()
        return c

    lax.fori_loop(1, 8, ret_wait, 0)
    rv = ret[...]
    out_ref[...] = (
        rs[...].astype(F32)
        + wa * jnp.dot(back[0], rv, preferred_element_type=F32)
        + wb * jnp.dot(back[1], rv, preferred_element_type=F32)
    ).astype(BF16)

    for m in sent1 + ag_sent + sent2:
        m.wait_send()

    def stat_sent(k, c):
        stat(k).wait_send()
        return c

    def deal_sent(k, c):
        deal(k).wait_send()
        return c

    lax.fori_loop(1, 16, stat_sent, 0)
    lax.fori_loop(1, 8, deal_sent, 0)
    for slot in range(8):
        if slot < 2:

            @pl.when(gc != slot)
            def _():
                back_copy(slot).wait_send()

        else:
            back_copy(slot).wait_send()


def layer(part, residual_in, norm_gain, router_weight, routes, gate_weight, up_weight, down_weight):
    vm = pl.BlockSpec(memory_space=pltpu.VMEM)
    hb = pl.BlockSpec(memory_space=pl.ANY)
    dma = pltpu.SemaphoreType.DMA
    return pl.pallas_call(
        layer_kernel,
        out_shape=jax.ShapeDtypeStruct((128, CW), BF16),
        in_specs=[vm, vm, vm, vm, vm, hb, hb, hb],
        out_specs=vm,
        scratch_shapes=[
            pltpu.VMEM((16 * CW, FW), BF16),
            pltpu.VMEM((16 * CW, FW), BF16),
            pltpu.VMEM((FW, 16 * CW), BF16),
            pltpu.VMEM((16, 512, CW), BF16),
            pltpu.VMEM((2, 2, 256, FW), F32),
            pltpu.VMEM((2, 256, 128), F32),
            pltpu.VMEM((2, 256, FW), BF16),
            pltpu.VMEM((16, 512, CW), BF16),
            pltpu.VMEM((2, 4, 6, 32, CW), BF16),
            pltpu.VMEM((2, 4, 64, CW), BF16),
            pltpu.VMEM((2, 6, 32, CW), BF16),
            pltpu.VMEM((2, 4, 6, 128, CW), BF16),
            pltpu.VMEM((2, 4, 256, CW), BF16),
            pltpu.VMEM((2, 6, 128, CW), BF16),
            pltpu.VMEM((128, CW), BF16),
            pltpu.VMEM((128, CW), BF16),
            pltpu.VMEM((8, 64, CW), BF16),
            pltpu.VMEM((512, CW), BF16),
            pltpu.VMEM((512, CW), BF16),
            pltpu.VMEM((8, 128), F32),
            pltpu.VMEM((16, 8, 128), F32),
            pltpu.VMEM((512, 128), BF16),
            pltpu.VMEM((2, 128, 512), BF16),
            dma((3,)),
            dma((60,)),
            dma((60,)),
            dma((60,)),
            dma((60,)),
            dma((60,)),
            dma((60,)),
            dma((8,)),
            dma((8,)),
            dma((8,)),
            dma((8,)),
            dma((16,)),
            dma((16,)),
        ],
        compiler_params=pltpu.CompilerParams(
            collective_id=0, has_side_effects=True, vmem_limit_bytes=60 * 1024 * 1024
        ),
        cost_estimate=pl.CostEstimate(flops=10 << 30, bytes_accessed=24 << 20, transcendentals=1 << 18),
        name="layer",
    )(
        part,
        residual_in,
        norm_gain.reshape(16, CW),
        router_weight.reshape(16, CW, 8),
        routes,
        gate_weight,
        up_weight,
        down_weight,
    )


def local(
    queries, new_kv, kv_cache, page_table, context_lengths, out_weight, residual_in,
    norm_gain, router_weight, routes, gate_weight, up_weight, down_weight,
):
    part = attention_partials(queries, new_kv, kv_cache, page_table, context_lengths, out_weight)
    return layer(part, residual_in, norm_gain, router_weight, routes, gate_weight, up_weight, down_weight)


def solution(mesh):
    return jax.shard_map(
        local,
        mesh=mesh,
        in_specs=(
            P("grp", "tp"),
            P("grp", "tp", None),
            P("grp", "tp", None, None),
            P("grp", None),
            P("grp"),
            P("tp", None),
            P("grp", "tp"),
            P(),
            P(),
            P("grp", None),
            P("grp", None, "tp"),
            P("grp", None, "tp"),
            P("grp", "tp", None),
        ),
        out_specs=P("grp", "tp"),
        check_vma=False,
    )
```

time: 391 us -> 160 us (0.41)
  waiting for transfers between devices: 220 us -> 0 us
  Pallas kernels: 0 us -> 146 us
  blocking collectives: 78.4 us -> 0 us
  matrix products: 31 us -> 0 us
  local copies, waits for them, and re-layouts: 34.9 us -> 13.7 us
  between operations: 13.4 us -> 0.03 us
  other arithmetic: 6.14 us -> 0 us
  starting transfers between devices: 6.13 us -> 0 us
    pallas_call x0 -> x2, Pallas kernels: none -> 146 us  [the longest x1 130 us: layer(): pl.pallas_call(layer_kernel, out_shape=jax.ShapeDtypeStruct((128, CW), BF...]
    psum x1 -> x0, waiting for transfers between devices: 88.1 us -> none  [local(): lax.psum(partial_value.astype(jnp.bfloat16), 'tp').astype(jnp.float32)]
    unnamed x4 -> x0, waiting for transfers between devices: 78.9 us -> none
    all_to_all x1 -> x0, blocking collectives: 78.4 us -> none  [local(): lax.all_to_all(outgoing.reshape(experts, capacity, model_width), 'grp', s...]
    all_gather x1 -> x0, waiting for transfers between devices: 47.1 us -> none  [local(): features = lax.all_gather(residual_in, 'tp', axis=1, tiled=True)]
    dot_general x10 -> x0, matrix products: 31 us -> none  [the longest x1 5.81 us: attention_rows(): jnp.einsum('rhd,rld->rhl', query_heads, gathered[:, :, :head_dim], prefer...]
    gather x1 -> x0, local copies, waits for them, and re-layouts: 19.3 us -> none  [attention_rows(): kv_cache[page_table.reshape(-1), 0]]
    all_to_all x1 -> x0, waiting for transfers between devices: 6.16 us -> none  [local(): lax.all_to_all(expert_rows.reshape(sources, capacity, col_width).astype(j...]
  transfers between devices with their start and end apart: 4 -> 0, of which waited for: 4 -> 0; matrix products, arithmetic and copies ran while one was open for 1% -> 0% of each run, Pallas kernels for 0% -> 0%
where the time goes in v1:
time: 160 us
  Pallas kernels  146 us (91%)
  local copies, waits for them, and re-layouts  13.7 us (9%)
    pallas_call x1, Pallas kernels, layer(): pl.pallas_call(layer_kernel, out_shape=jax.ShapeDtypeStruct((128, CW), BF...  130 us
    pallas_call x1, Pallas kernels, attention_partials(): pl.pallas_call(attn_kernel, out_shape=jax.ShapeDtypeStruct((16, 128, 384)...  15.6 us
    unnamed x19, local copies, waits for them, and re-layouts  12.4 us

profile of v1, /device:TPU:1, one launch (start us, length us, event | category | flops | bytes accessed | tf_op | source)
XLA Modules:
  0.0 159.8 jit_solution(14763748479203179379)
XLA Ops:
  0.0 1.3 reshape.18.gain_ref
  1.3 1.4 copy.15.routes_ref
  2.8 0.0 copy-start
  2.8 1.9 %copy-done = bf16[400,1,16,256]{3,2,1,0:T(8,128)(2,1)S(1)} copy-done((bf16[400,1,16,256]{3,2,1,0:T(8,128)(2,1)S(1)}, bf16[400,1,16,256]{3,2,1,0:T(8,128)(2,1)}, u32[]{:S(2)}) %copy-start) | copy-done | bytes 3276824
  4.7 0.0 copy-start.1
  4.7 1.9 %copy-done.1 = bf16[256,6144]{1,0:T(8,128)(2,1)S(1)} copy-done((bf16[256,6144]{1,0:T(8,128)(2,1)S(1)}, bf16[256,6144]{1,0:T(8,128)(2,1)}, u32[]{:S(2)}) %copy-start.1) | copy-done | bytes 3145752
  6.6 0.0 copy-start.3
  6.6 0.8 copy-done.3
  7.4 0.0 copy-start.4
  7.4 0.8 copy-done.4
  8.3 0.0 copy-start.5
  8.3 0.7 copy-done.5
  9.0 0.0 copy-start.6
  9.0 0.7 copy-done.6
  9.6 0.0 copy-start.7
  9.6 15.6 %attention.1.part_ref = bf16[16,128,384]{2,1,0:T(8,128)(2,1)S(1)} custom-call(bf16[128,256]{1,0:T(8,128)(2,1)S(1)} %copy-done.3, bf16[128,256]{1,0:T(8,128)(2,1)S(1)} %bitcast.6, s32[16,128]{1,0:T(8,128)S(1)} %bitcast.7, s32[1,128]{1,0:T(1,128)S(1)} %bitcast.8, bf16[6400,256]{1,0:T(8,128)(2,1)S(1)} %bitcast.5, bf16[256,6144]{1,0:T(8,128)(2,1)S(1)} %copy-done.1), custom_call_target="tpu_custom_call" | custom-call | flops 1073741824 | bytes 8388608 | tf_op jit(solution)/shard_map/attention/pallas_call | solution.py:102
  25.2 0.0 copy-start.2
  25.3 1.1 copy-done.2
  26.4 0.0 copy-done.7
  26.4 1.5 copy.14
  27.9 130.4 %layer.1 = bf16[128,384]{1,0:T(8,128)(2,1)} custom-call(bf16[16,128,384]{2,1,0:T(8,128)(2,1)} %copy-done.2, bf16[128,384]{1,0:T(8,128)(2,1)} %res_ref.1, f32[16,384]{1,0:T(8,128)} %reshape.18.gain_ref, bf16[16,384,8]{2,1,0:T(8,128)(2,1)} %bitcast.9, s32[128,2]{1,0:T(8,128)} %copy.15.routes_ref, bf16[1,6144,512]{2,1,0:T(8,128)(2,1)} %wg_hbm.1, ...), custom_call_target="tpu_custom_call" | custom-call | flops 10737418240 | bytes 25165824 | tf_op jit(solution)/shard_map/layer/pallas_call | solution.py:604
  158.2 1.5 copy.17
Async XLA Ops:
  2.8 1.9 %copy-start = (bf16[400,1,16,256]{3,2,1,0:T(8,128)(2,1)S(1)}, bf16[400,1,16,256]{3,2,1,0:T(8,128)(2,1)}, u32[]{:S(2)}) copy-start(bf16[400,1,16,256]{3,2,1,0:T(8,128)(2,1)} %param.15) | copy-start | bytes 9830404
  4.7 1.9 %copy-start.1 = (bf16[256,6144]{1,0:T(8,128)(2,1)S(1)}, bf16[256,6144]{1,0:T(8,128)(2,1)}, u32[]{:S(2)}) copy-start(bf16[256,6144]{1,0:T(8,128)(2,1)} %w_hbm.1) | copy-start | bytes 9437188
  6.6 0.8 copy-start.3
  7.4 0.8 copy-start.4
  8.3 0.7 copy-start.5
  9.0 0.7 copy-start.6
  9.6 16.8 %copy-start.7 = (bf16[6144,8]{0,1:T(8,128)(2,1)S(1)}, bf16[6144,8]{0,1:T(8,128)(2,1)}, u32[]{:S(2)}) copy-start(bf16[6144,8]{0,1:T(8,128)(2,1)} %param.21) | copy-start | bytes 294916
  25.2 1.1 copy-start.2

commit v2 on v1

v2 whole, which is shorter than its diff:
```python
import jax
import jax.numpy as jnp
from jax import lax
from jax.experimental import pallas as pl
from jax.experimental.pallas import tpu as pltpu
from jax.sharding import PartitionSpec as P

F32 = jnp.float32
BF16 = jnp.bfloat16
MESH = pl.DeviceIdType.MESH
NT = (((1,), (1,)), ((), ()))
TN = (((0,), (0,)), ((), ()))
PARTS = 5
NEG = -1e30
CW = 384
FW = 512
OFFS_OUT = (0, 3, 1, 2)
OFFS_IN = (2, 1, 3, 0)


def attend(q, own, live_ref, kv, kv_copies, part_rows):
    q2 = jnp.concatenate([q[:, :128], q[:, 128:]], axis=0)
    pages = part_rows // 16
    tok = lax.broadcasted_iota(jnp.int32, (256, 128), 0)
    offs = (tok & 15).astype(F32)
    tok16 = lax.broadcasted_iota(jnp.int32, (256, 16), 0) >> 4
    spread = (tok16 == lax.broadcasted_iota(jnp.int32, (256, 16), 1)).astype(F32).astype(BF16)
    s_own = lax.dot_general(own[:, :128], q2, NT, preferred_element_type=F32)
    row = lax.broadcasted_iota(jnp.int32, (128, 128), 0)
    col = lax.broadcasted_iota(jnp.int32, (128, 128), 1)
    eye = (row == col).astype(F32)
    eye = jnp.concatenate([eye, eye], axis=1)
    top = jnp.sum(s_own * eye, axis=0, keepdims=True)
    tot = jnp.ones((8, 256), F32) * 0.125
    own_v = jnp.transpose(own[:, 128:].astype(F32))
    acc = jnp.concatenate([own_v, own_v], axis=1)
    scale = 128.0 ** -0.5
    for i, copy in enumerate(kv_copies):
        copy.wait()
        tiles = []
        peak = top
        for c in range(part_rows // 256):
            at = i * part_rows + c * 256
            s = lax.dot_general(kv[at : at + 256, :128], q2, NT, preferred_element_type=F32)
            cn = live_ref[i * pages + c * 16 : i * pages + c * 16 + 16, :]
            m = offs < jnp.dot(spread, cn, preferred_element_type=F32)
            s = jnp.concatenate([jnp.where(m, s[:, :128], NEG), jnp.where(m, s[:, 128:], NEG)], axis=1)
            tiles.append(s)
            peak = jnp.maximum(peak, jnp.max(jnp.max(s.reshape(32, 8, 256), axis=0), axis=0, keepdims=True))
        fade = jnp.exp((top - peak) * scale)
        top = peak
        tot = tot * fade
        ps = []
        for s in tiles:
            p = jnp.exp((s - top) * scale)
            tot = tot + jnp.sum(p.reshape(32, 8, 256), axis=0)
            ps.append(p.astype(BF16))
        p = jnp.concatenate(ps, axis=0)
        acc = acc * fade + lax.dot_general(
            kv[i * part_rows : (i + 1) * part_rows, 128:], p, TN, preferred_element_type=F32
        )
    att = acc / jnp.sum(tot, axis=0, keepdims=True)
    return jnp.concatenate([jnp.transpose(att[:, :128]), jnp.transpose(att[:, 128:])], axis=1).astype(BF16)


def as_column(row):
    return jnp.transpose(jnp.broadcast_to(row, (128, 128)))[:, 0:1]


def route_maps(routes):
    lane = lax.broadcasted_iota(jnp.int32, (128, 128), 1)
    sub = lax.broadcasted_iota(jnp.int32, (128, 128), 0)
    hit0 = (sub == routes[0:1, :]).astype(F32)
    hit1 = (sub == routes[1:2, :]).astype(F32)
    hit = hit0 + hit1
    rank = jnp.dot(hit.astype(BF16), (sub < lane).astype(F32).astype(BF16), preferred_element_type=F32)
    spot = jnp.where(hit > 0.5, rank, -1.0)
    slot = lax.broadcasted_iota(jnp.int32, (64, 128), 0).astype(F32)
    place = jnp.concatenate([(slot == spot[e : e + 1, :]).astype(F32) for e in range(8)], axis=0)
    wide = lax.broadcasted_iota(jnp.int32, (128, 512), 1).astype(F32)

    def back(h, r):
        at = r.astype(F32) * 64.0 + jnp.sum(h * rank, axis=0, keepdims=True)
        return (wide == as_column(at)).astype(F32).astype(BF16)

    sign = hit0[:8, :] - hit1[:8, :]
    return place.astype(BF16), back(hit0, routes[0:1, :]), back(hit1, routes[1:2, :]), sign


def layer_kernel(
    q_hbm, own_hbm, pt_hbm, len_hbm, kv_hbm, w_hbm, res_hbm, gain_hbm, router_hbm, routes_hbm, wg_hbm, wu_hbm, wd_hbm,
    out_ref,
    q_ref, own_ref, pt_ref, len_ref, kv, w, res_ref, gain_ref, router_ref, routes_ref, live, part, ginv,
    wg, wu, wd, xg, acc, ssq, hid, p2, rb1, y1, rc1, rb2, y2, rc2,
    rs, xs, ds, fin, ret, stat_out, stat_in, place, back,
    ksem, msem, wsem, a1s, a1r, ags, agr, a2s, a2r, ds_s, ds_r, rt_s, rt_r, st_s, st_r,
):
    g = lax.axis_index("grp")
    t = lax.axis_index("tp")
    gy, gc = g // 2, lax.rem(g, 2)
    tz, tx = t // 4, lax.rem(t, 4)
    me = ((tx, tz), (tz, tx))

    def tid(h, c1, c2):
        return c2 * 4 + c1 if h == 0 else c1 * 4 + c2

    def m4(v):
        return lax.rem(v + 4, 4)

    barrier = pltpu.get_barrier_semaphore()

    def greet_t(k, c):
        pl.semaphore_signal(barrier, inc=1, device_id=(g, lax.rem(t + k, 16)), device_id_type=MESH)
        return c

    def greet_g(k, c):
        pl.semaphore_signal(barrier, inc=1, device_id=(lax.rem(g + k, 8), t), device_id_type=MESH)
        return c

    lax.fori_loop(1, 16, greet_t, 0)
    lax.fori_loop(1, 8, greet_g, 0)

    step = kv.shape[0] // PARTS
    small = [
        pltpu.make_async_copy(src, dst, msem.at[i])
        for i, (src, dst) in enumerate(
            (
                (pt_hbm, pt_ref), (len_hbm, len_ref), (q_hbm, q_ref), (own_hbm, own_ref), (routes_hbm, routes_ref),
                (res_hbm, res_ref), (gain_hbm, gain_ref), (router_hbm, router_ref), (w_hbm, w),
            )
        )
    ]
    kv_copies = [
        pltpu.make_async_copy(kv_hbm.at[pl.ds(i * step, step)], kv.at[pl.ds(i * step, step)], ksem.at[i])
        for i in range(PARTS)
    ]
    wcopies = [
        pltpu.make_async_copy(src.at[0], dst, wsem.at[i])
        for i, (src, dst) in enumerate(((wg_hbm, wg), (wu_hbm, wu), (wd_hbm, wd)))
    ]
    for c in small[:5] + kv_copies + small[5:] + wcopies:
        c.start()

    small[0].wait()
    small[1].wait()
    pages = live.shape[0]
    page_ids = lax.broadcasted_iota(jnp.int32, (pages, 128), 0)
    lens = len_ref[...]
    count = jnp.zeros((pages, 128), jnp.int32)
    for j in range(16):
        here = jnp.clip(lens - 16 * j, 0, 16)
        count = count + jnp.where(page_ids == pt_ref[j : j + 1, :], here, 0)
    live[...] = count.astype(F32).astype(BF16)
    small[4].wait()
    pl_m, b0, b1, sign = route_maps(routes_ref[...])
    place[...] = pl_m
    back[0] = b0
    back[1] = b1
    small[2].wait()
    small[3].wait()
    attn = attend(q_ref[...], own_ref[...], live, kv, kv_copies, step)
    for c in small[5:]:
        c.wait()
    ginv[...] = 1.0 / gain_ref[...]

    pl.semaphore_wait(barrier, 22)

    def rcopy(src, dst, ss, rr, dev):
        return pltpu.make_async_remote_copy(
            src_ref=src, dst_ref=dst, send_sem=ss, recv_sem=rr, device_id=dev, device_id_type=MESH
        )

    def reduce_scatter(rows, src, rb, y, rc, ss, rr, produce, finish):
        def q_rows(h, q):
            return pl.ds((2 * h + q) * rows, rows)

        def nbr(h, axis, d):
            c = list(me[h])
            c[axis] = m4(c[axis] + d)
            return (g, tid(h, c[0], c[1]))

        def blk(h, i, d2):
            return tid(h, m4(me[h][0] + OFFS_IN[i]), m4(me[h][1] + d2))

        def msg1(h, i, k, from_buf=None):
            d2, q, d = ((2, 0, 1), (2, 1, -1), (1, 1, 1), (-1, 0, -1), (1, 0, 1), (-1, 1, -1))[k]
            s = src.at[blk(h, i, d2), q_rows(h, q)] if from_buf is None else rb.at[h, i, from_buf]
            n = h * 24 + i * 6 + k
            return rcopy(s, rb.at[h, i, k], ss.at[n], rr.at[n], nbr(h, 1, d))

        def msg2(h, k, i, from_buf=None):
            q, d = ((0, 1), (1, -1), (1, 1), (0, -1), (0, 1), (1, -1))[k]
            s = y.at[h, i, pl.ds(q * rows, rows)] if from_buf is None else rc.at[h, from_buf]
            n = 48 + h * 6 + k
            return rcopy(s, rc.at[h, k], ss.at[n], rr.at[n], nbr(h, 0, d))

        sent = []

        def go(m):
            m.start()
            sent.append(m)

        def stage_g(i):
            produce(i, blk, 0)
            for h in (0, 1):
                go(msg1(h, i, 0))
                go(msg1(h, i, 1))
            produce(i, blk, 1)
            for h in (0, 1):
                go(msg1(h, i, 2))
                go(msg1(h, i, 3))

        def stage_h(i):
            for h in (0, 1):
                msg1(h, i, 0).wait_recv()
                rb[h, i, 0] = (
                    rb[h, i, 0].astype(F32) + src[blk(h, i, 1), q_rows(h, 0)].astype(F32)
                ).astype(BF16)
                go(msg1(h, i, 4, 0))
                msg1(h, i, 1).wait_recv()
                rb[h, i, 1] = (
                    rb[h, i, 1].astype(F32) + src[blk(h, i, -1), q_rows(h, 1)].astype(F32)
                ).astype(BF16)
                go(msg1(h, i, 5, 1))

        def stage_j(i):
            produce(i, blk, 2)
            for h in (0, 1):
                for q, (k1, k2) in ((0, (3, 4)), (1, (2, 5))):
                    msg1(h, i, k1).wait_recv()
                    msg1(h, i, k2).wait_recv()
                    y[h, i, pl.ds(q * rows, rows)] = (
                        src[blk(h, i, 0), q_rows(h, q)].astype(F32)
                        + rb[h, i, k1].astype(F32)
                        + rb[h, i, k2].astype(F32)
                    ).astype(BF16)
                    if i == 0:
                        go(msg2(h, q, 0))
                if i == 1:
                    go(msg2(h, 2, 1))
                    msg2(h, 0, 1).wait_recv()
                    rc[h, 0] = (rc[h, 0].astype(F32) + y[h, 1, pl.ds(0, rows)].astype(F32)).astype(BF16)
                    go(msg2(h, 4, 1, 0))
                if i == 2:
                    go(msg2(h, 3, 2))
                    msg2(h, 1, 2).wait_recv()
                    rc[h, 1] = (rc[h, 1].astype(F32) + y[h, 2, pl.ds(rows, rows)].astype(F32)).astype(BF16)
                    go(msg2(h, 5, 2, 1))

        stage_g(0)
        stage_g(1)
        stage_h(0)
        stage_g(2)
        stage_h(1)
        stage_j(0)
        stage_g(3)
        stage_h(2)
        stage_j(1)
        stage_h(3)
        stage_j(2)
        stage_j(3)
        for h in (0, 1):
            for q, (k1, k2) in ((0, (3, 4)), (1, (2, 5))):
                msg2(h, k1, 3).wait_recv()
                msg2(h, k2, 3).wait_recv()
                finish(
                    h,
                    q,
                    y[h, 3, pl.ds(q * rows, rows)].astype(F32)
                    + rc[h, k1].astype(F32)
                    + rc[h, k2].astype(F32),
                )
        return sent

    sent1 = []

    def project(n, c):
        def third(v):
            return v + (v == 2).astype(jnp.int32)

        m = n - 7
        ox = jnp.where(n < 4, 2, jnp.where(n < 7, third(n - 4), third(m // 3)))
        oz = jnp.where(n < 4, n, jnp.where(n < 7, 2, third(lax.rem(m, 3))))
        b = m4(tz + oz) * 4 + m4(tx + ox)
        part[b] = jnp.dot(
            attn, w[:, pl.ds(pl.multiple_of(b * CW, 128), CW)], preferred_element_type=F32
        ).astype(BF16)
        return c

    def far(h, axis, o):
        c = list(me[h])
        c[axis] = m4(c[axis] + o)
        return (g, tid(h, c[0], c[1]))

    def out1(h, i, k):
        o1, o2 = OFFS_IN[i], (2, 1, -1)[k]
        n = h * 12 + i * 3 + k
        return rcopy(
            part.at[tid(h, m4(me[h][0] + o1), m4(me[h][1] + o2)), pl.ds(h * 64, 64)],
            rb1.at[h, i, k], a1s.at[n], a1r.at[n], far(h, 1, o2),
        )

    def out2(h, i):
        n = 24 + h * 3 + i
        return rcopy(y1.at[h, i], rc1.at[h, i], a1s.at[n], a1r.at[n], far(h, 0, OFFS_IN[i]))

    def go1(m):
        m.start()
        sent1.append(m)

    lax.fori_loop(0, 7, project, 0)
    for k in range(3):
        for h in (0, 1):
            go1(out1(h, 0, k))
    lax.fori_loop(7, 16, project, 0)
    for i in (1, 2, 3):
        for k in range(3):
            for h in (0, 1):
                go1(out1(h, i, k))
    gain_row = gain_ref[:, pl.ds(pl.multiple_of(t * CW, 128), CW)]
    for i in range(4):
        for h in (0, 1):
            for k in range(3):
                out1(h, i, k).wait_recv()
            v = part[tid(h, m4(me[h][0] + OFFS_IN[i]), me[h][1]), h * 64 : h * 64 + 64, :].astype(F32)
            for k in range(3):
                v = v + rb1[h, i, k].astype(F32)
            if i < 3:
                y1[h, i] = v.astype(BF16)
                go1(out2(h, i))
            else:
                for k in range(3):
                    out2(h, k).wait_recv()
                    v = v + rc1[h, k].astype(F32)
                at = pl.ds(h * 64, 64)
                r = (res_ref[at, :].astype(F32) + v).astype(BF16)
                rs[at, :] = r
                xs[at, :] = (r.astype(F32) * gain_row).astype(BF16)

    x = xs[...]
    ds[...] = jnp.dot(place[...], x, preferred_element_type=F32).astype(BF16).reshape(8, 64, CW)

    def seat(src_y, src_c, dst_y):
        r = m4(src_y - dst_y)
        p = lax.rem(r, 2) * 2 + r // 2
        return pl.multiple_of(p * 128 + src_c * 64, 64), p * 2 + src_c

    own_row, own_slot = seat(gy, gc, gy)
    xg[t, pl.ds(own_row, 64), :] = ds[g]

    def deal(k):
        e = lax.rem(g + k, 8)
        row, slot = seat(gy, gc, e // 2)
        return rcopy(ds.at[e], xg.at[t, pl.ds(row, 64)], ds_s.at[k], ds_r.at[slot], (e, t))

    def deal_start(k, c):
        deal(k).start()
        return c

    lax.fori_loop(1, 8, deal_start, 0)

    def dealt(slot):
        at = xg.at[t, pl.ds(pl.multiple_of(slot * 64, 64), 64)]
        return rcopy(at, at, ds_s.at[0], ds_r.at[slot], (g, t))

    logit = lax.dot_general(
        router_ref[:, pl.ds(pl.multiple_of(t * CW, 128), CW)], x, NT, preferred_element_type=F32
    )
    diff = jnp.sum(logit * sign, axis=0, keepdims=True)
    r32 = rs[...].astype(F32)
    sq = jnp.sum(r32 * r32, axis=1, keepdims=True)
    sq = jnp.transpose(jnp.broadcast_to(sq, (128, 128)))[:8, :]
    sub8 = lax.broadcasted_iota(jnp.int32, (8, 128), 0)
    tile = jnp.where(sub8 == 0, diff, jnp.where(sub8 == 1, sq, 0.0))
    stat_out[...] = tile
    stat_in[0] = tile

    def stat(k):
        return rcopy(stat_out, stat_in.at[k], st_s.at[k], st_r.at[k], (g, lax.rem(t + k, 16)))

    def stat_start(k, c):
        stat(k).start()
        return c

    lax.fori_loop(1, 16, stat_start, 0)

    ag_sent = []

    def ag(h, phase, i, k, b):
        q, d = ((0, 1), (1, 1), (0, -1), (1, -1), (0, 1), (1, -1))[k]
        c = list(me[h])
        c[phase] = m4(c[phase] + d)
        ref = xg.at[b, pl.ds((2 * h + q) * 128, 128)]
        n = h * 30 + phase * 6 + i * 6 + k
        return rcopy(ref, ref, ags.at[n], agr.at[n], (g, tid(h, c[0], c[1])))

    def send(*a):
        m = ag(*a)
        m.start()
        ag_sent.append(m)

    def ab(h, o1, o2):
        return tid(h, m4(me[h][0] + o1), m4(me[h][1] + o2))

    def wait(h, phase, i, k, b):
        ag(h, phase, i, k, b).wait_recv()

    def spread(h, i, q):
        b = ab(h, OFFS_OUT[i], 0)
        send(h, 1, i, q, b)
        send(h, 1, i, 2 + q, b)

    def own_quarter(h, q):
        p = 2 * h + q
        for c in (0, 1):
            slot = p * 2 + c
            if p == 0:

                @pl.when(gc != c)
                def _():
                    dealt(slot).wait_recv()

            else:
                dealt(slot).wait_recv()
        send(h, 0, 0, q, t)
        send(h, 0, 0, 2 + q, t)

    def stage_f(i):
        for h in (0, 1):
            b = ab(h, OFFS_OUT[i], -1)
            wait(h, 1, i, 0, b)
            send(h, 1, i, 4, b)
            b = ab(h, OFFS_OUT[i], 1)
            wait(h, 1, i, 3, b)
            send(h, 1, i, 5, b)

    def stage_w1(i):
        for h in (0, 1):
            wait(h, 1, i, 1, ab(h, OFFS_OUT[i], -1))
            wait(h, 1, i, 2, ab(h, OFFS_OUT[i], 1))

    def stage_w2(i):
        for h in (0, 1):
            b = ab(h, OFFS_OUT[i], 2)
            wait(h, 1, i, 4, b)
            wait(h, 1, i, 5, b)

    def eat(*offsets):
        def body(n, c):
            h = lax.rem(n, 2)
            j = n // 2
            o1, o2 = offsets[0]
            for m, (u1, u2) in enumerate(offsets):
                o1 = jnp.where(j == m, u1, o1)
                o2 = jnp.where(j == m, u2, o2)
            c1 = m4(jnp.where(h == 0, tx, tz) + o1)
            c2 = m4(jnp.where(h == 0, tz, tx) + o2)
            b = jnp.where(h == 0, c2 * 4 + c1, c1 * 4 + c2)
            xb = xg[b, pl.ds(pl.multiple_of(h * 256, 256), 256), :]
            wat = pl.ds(pl.multiple_of(b * CW, CW), CW)
            acc[h, 0] += jnp.dot(xb, wg[wat, :], preferred_element_type=F32)
            acc[h, 1] += jnp.dot(xb, wu[wat, :], preferred_element_type=F32)
            v = xb.astype(F32) * ginv[:, pl.ds(pl.multiple_of(b * CW, 128), CW)]
            v = v * v
            ssq[h] += v[:, :128] + v[:, 128:256] + v[:, 256:]
            return c

        lax.fori_loop(0, len(offsets) * 2, body, 0)

    own_quarter(0, 0)
    spread(0, 0, 0)
    own_quarter(1, 0)
    own_quarter(1, 1)
    own_quarter(0, 1)
    spread(1, 0, 0)
    spread(1, 0, 1)
    spread(0, 0, 1)
    acc[...] = jnp.zeros_like(acc)
    ssq[...] = jnp.zeros_like(ssq)

    lo = [ab(h, -1, 0) for h in (0, 1)]
    hi = [ab(h, 1, 0) for h in (0, 1)]
    wait(0, 0, 0, 0, lo[0])
    send(0, 0, 0, 4, lo[0])
    spread(0, 1, 0)
    wait(0, 0, 0, 2, hi[0])
    spread(0, 2, 0)
    wait(1, 0, 0, 0, lo[1])
    send(1, 0, 0, 4, lo[1])
    wait(1, 0, 0, 3, hi[1])
    send(1, 0, 0, 5, hi[1])
    wait(0, 0, 0, 3, hi[0])
    send(0, 0, 0, 5, hi[0])
    spread(1, 1, 0)
    spread(1, 2, 1)
    spread(0, 2, 1)
    wait(0, 0, 0, 1, lo[0])
    spread(0, 1, 1)
    wait(1, 0, 0, 1, lo[1])
    spread(1, 1, 1)
    wait(1, 0, 0, 2, hi[1])
    spread(1, 2, 0)
    wcopies[0].wait()
    wcopies[1].wait()
    eat((0, 0))
    stage_f(0)
    for h in (0, 1):
        b = ab(h, 2, 0)
        wait(h, 0, 0, 4, b)
        spread(h, 3, 0)
        wait(h, 0, 0, 5, b)
        spread(h, 3, 1)
    eat((3, 0), (1, 0))
    stage_f(1)
    stage_w1(0)
    eat((2, 0), (0, 3), (0, 1))
    stage_f(2)
    stage_w1(1)
    eat((3, 3), (3, 1))
    stage_w2(0)
    eat((0, 2))
    stage_f(3)
    stage_w1(2)
    stage_w2(1)
    eat((1, 3), (1, 1), (3, 2))
    stage_w1(3)
    eat((2, 3), (2, 1))
    stage_w2(2)
    eat((1, 2))
    stage_w2(3)
    eat((2, 2))

    for h in (0, 1):
        total = jnp.sum(ssq[h], axis=1, keepdims=True)
        sc = lax.rsqrt(total / (16.0 * CW) + 1e-5)
        gate = acc[h, 0] * sc
        up = acc[h, 1] * sc
        hid[h] = (gate / (1.0 + jnp.exp(-gate)) * up).astype(BF16)
    wcopies[2].wait()

    def produce(i, blk, stage):
        todo = ((2,), (1, -1), (0,))[stage]
        for h in (0, 1):
            hv = hid[h]
            for d2 in todo:
                b = blk(h, i, d2)
                p2[b, h * 256 : (h + 1) * 256, :] = jnp.dot(
                    hv, wd[:, pl.ds(pl.multiple_of(b * CW, 128), CW)], preferred_element_type=F32
                ).astype(BF16)

    def back_copy(slot):
        p = slot // 2
        r = lax.rem(p, 2) * 2 + p // 2
        dst = lax.rem(gy + r, 4) * 2 + lax.rem(slot, 2)
        return rcopy(
            fin.at[pl.ds(pl.multiple_of(slot * 64, 64), 64)],
            ret.at[pl.ds(pl.multiple_of(g * 64, 64), 64)],
            rt_s.at[slot],
            rt_r.at[g],
            (dst, t),
        )

    def finish2(h, q, v):
        p = 2 * h + q
        fin[p * 128 : (p + 1) * 128, :] = v.astype(BF16)
        for c in (0, 1):
            slot = p * 2 + c
            if p == 0:

                @pl.when(gc != c)
                def _():
                    back_copy(slot).start()

                @pl.when(gc == c)
                def _():
                    ret[pl.ds(pl.multiple_of(g * 64, 64), 64), :] = fin[slot * 64 : slot * 64 + 64, :]

            else:
                back_copy(slot).start()

    sent2 = reduce_scatter(128, p2, rb2, y2, rc2, a2s, a2r, produce, finish2)

    def stat_wait(k, c):
        stat(k).wait_recv()
        return c

    lax.fori_loop(1, 16, stat_wait, 0)
    sums = jnp.sum(stat_in[...], axis=0)
    diff_all = sums[0:1, :] * lax.rsqrt(sums[1:2, :] / (16.0 * CW) + 1e-5)
    dcol = as_column(diff_all)
    wa = 1.0 / (1.0 + jnp.exp(-dcol))
    wb = 1.0 / (1.0 + jnp.exp(dcol))

    def ret_wait(k, c):
        e = lax.rem(g + k, 8)
        at = ret.at[pl.ds(pl.multiple_of(e * 64, 64), 64)]
        rcopy(at, at, rt_s.at[0], rt_r.at[e], (g, t)).wait_recv()
        return c

    lax.fori_loop(1, 8, ret_wait, 0)
    rv = ret[...]
    out_ref[...] = (
        rs[...].astype(F32)
        + wa * jnp.dot(back[0], rv, preferred_element_type=F32)
        + wb * jnp.dot(back[1], rv, preferred_element_type=F32)
    ).astype(BF16)

    for m in sent1 + ag_sent + sent2:
        m.wait_send()

    def stat_sent(k, c):
        stat(k).wait_send()
        return c

    def deal_sent(k, c):
        deal(k).wait_send()
        return c

    lax.fori_loop(1, 16, stat_sent, 0)
    lax.fori_loop(1, 8, deal_sent, 0)
    for slot in range(8):
        if slot < 2:

            @pl.when(gc != slot)
            def _():
                back_copy(slot).wait_send()

        else:
            back_copy(slot).wait_send()


def local(
    queries, new_kv, kv_cache, page_table, context_lengths, out_weight, residual_in,
    norm_gain, router_weight, routes, gate_weight, up_weight, down_weight,
):
    pool = kv_cache.shape[0] * kv_cache.shape[2]
    hb = pl.BlockSpec(memory_space=pl.ANY)
    dma = pltpu.SemaphoreType.DMA
    return pl.pallas_call(
        layer_kernel,
        out_shape=jax.ShapeDtypeStruct((128, CW), BF16),
        in_specs=[hb] * 13,
        out_specs=pl.BlockSpec(memory_space=pltpu.VMEM),
        scratch_shapes=[
            pltpu.VMEM((128, 256), BF16),
            pltpu.VMEM((128, 256), BF16),
            pltpu.VMEM((16, 128), jnp.int32),
            pltpu.VMEM((1, 128), jnp.int32),
            pltpu.VMEM((pool, 256), BF16),
            pltpu.VMEM((256, 16 * CW), BF16),
            pltpu.VMEM((128, CW), BF16),
            pltpu.VMEM((1, 16 * CW), F32),
            pltpu.VMEM((8, 16 * CW), BF16),
            pltpu.VMEM((2, 128), jnp.int32),
            pltpu.VMEM((pool // 16, 128), BF16),
            pltpu.VMEM((16, 128, CW), BF16),
            pltpu.VMEM((1, 16 * CW), F32),
            pltpu.VMEM((16 * CW, FW), BF16),
            pltpu.VMEM((16 * CW, FW), BF16),
            pltpu.VMEM((FW, 16 * CW), BF16),
            pltpu.VMEM((16, 512, CW), BF16),
            pltpu.VMEM((2, 2, 256, FW), F32),
            pltpu.VMEM((2, 256, 128), F32),
            pltpu.VMEM((2, 256, FW), BF16),
            pltpu.VMEM((16, 512, CW), BF16),
            pltpu.VMEM((2, 4, 3, 64, CW), BF16),
            pltpu.VMEM((2, 3, 64, CW), BF16),
            pltpu.VMEM((2, 3, 64, CW), BF16),
            pltpu.VMEM((2, 4, 6, 128, CW), BF16),
            pltpu.VMEM((2, 4, 256, CW), BF16),
            pltpu.VMEM((2, 6, 128, CW), BF16),
            pltpu.VMEM((128, CW), BF16),
            pltpu.VMEM((128, CW), BF16),
            pltpu.VMEM((8, 64, CW), BF16),
            pltpu.VMEM((512, CW), BF16),
            pltpu.VMEM((512, CW), BF16),
            pltpu.VMEM((8, 128), F32),
            pltpu.VMEM((16, 8, 128), F32),
            pltpu.VMEM((512, 128), BF16),
            pltpu.VMEM((2, 128, 512), BF16),
            dma((PARTS,)),
            dma((9,)),
            dma((3,)),
            dma((30,)),
            dma((30,)),
            dma((60,)),
            dma((60,)),
            dma((60,)),
            dma((60,)),
            dma((8,)),
            dma((8,)),
            dma((8,)),
            dma((8,)),
            dma((16,)),
            dma((16,)),
        ],
        compiler_params=pltpu.CompilerParams(
            collective_id=0, has_side_effects=True, vmem_limit_bytes=60 * 1024 * 1024
        ),
        cost_estimate=pl.CostEstimate(flops=11 << 30, bytes_accessed=26 << 20, transcendentals=1 << 21),
        name="layer",
    )(
        queries,
        new_kv.reshape(128, 256),
        page_table.T,
        context_lengths.reshape(1, 128),
        kv_cache.reshape(pool, 256),
        out_weight,
        residual_in,
        norm_gain.reshape(1, 16 * CW),
        router_weight.T,
        routes.T,
        gate_weight,
        up_weight,
        down_weight,
    )


def solution(mesh):
    return jax.shard_map(
        local,
        mesh=mesh,
        in_specs=(
            P("grp", "tp"),
            P("grp", "tp", None),
            P("grp", "tp", None, None),
            P("grp", None),
            P("grp"),
            P("tp", None),
            P("grp", "tp"),
            P(),
            P(),
            P("grp", None),
            P("grp", None, "tp"),
            P("grp", None, "tp"),
            P("grp", "tp", None),
        ),
        out_specs=P("grp", "tp"),
        check_vma=False,
    )
```

time: 160 us -> 115 us (0.72)
  Pallas kernels: 146 us -> 113 us
  local copies, waits for them, and re-layouts: 13.7 us -> 1.54 us
    pallas_call x2 -> x1, Pallas kernels: 146 us -> 113 us  [local(): pl.pallas_call(layer_kernel, out_shape=jax.ShapeDtypeStruct((128, CW), BF...]
    unnamed x19 -> x1, local copies, waits for them, and re-layouts: 12.4 us -> 1.54 us
where the time goes in v2:
time: 115 us
  Pallas kernels  113 us (98%)
  local copies, waits for them, and re-layouts  1.54 us (1%)
    pallas_call x1, Pallas kernels, local(): pl.pallas_call(layer_kernel, out_shape=jax.ShapeDtypeStruct((128, CW), BF...  113 us

profile of v2, /device:TPU:1, one launch (start us, length us, event | category | flops | bytes accessed | tf_op | source)
XLA Modules:
  0.0 114.7 jit_solution(7374172871190177973)
XLA Ops:
  0.0 113.2 %layer.1 = bf16[128,384]{1,0:T(8,128)(2,1)} custom-call(bf16[128,256]{1,0:T(8,128)(2,1)} %q_hbm.1, bf16[128,256]{1,0:T(8,128)(2,1)} %bitcast.9, s32[16,128]{1,0:T(8,128)} %bitcast.11, s32[1,128]{1,0:T(1,128)} %bitcast.13, bf16[6400,256]{1,0:T(8,128)(2,1)} %bitcast.7, bf16[256,6144]{1,0:T(8,128)(2,1)} %w_hbm.1, bf16[128,384]{1,0:T(8,128)(2,1)} %res_hbm.1, ...), custom_call_target="tpu_custom_call" | custom-call | flops 11811160064 | bytes 27262976 | tf_op jit(solution)/shard_map/layer/pallas_call | solution.py:639
  113.2 1.5 %copy.15 = bf16[128,384]{1,0:T(8,128)(2,1)} copy(bf16[128,384]{1,0:T(8,128)(2,1)} %layer.1) | data formatting | bytes 196608

commit v3 on v2

--- a/solution.py
+++ b/solution.py
@@ -92,7 +92,7 @@
     out_ref,
     q_ref, own_ref, pt_ref, len_ref, kv, w, res_ref, gain_ref, router_ref, routes_ref, live, part, ginv,
     wg, wu, wd, xg, acc, ssq, hid, p2, rb1, y1, rc1, rb2, y2, rc2,
-    rs, xs, ds, fin, ret, stat_out, stat_in, place, back,
+    rs, xs, ds, ret, stat_out, stat_in, place, back,
     ksem, msem, wsem, a1s, a1r, ags, agr, a2s, a2r, ds_s, ds_r, rt_s, rt_r, st_s, st_r,
 ):
     g = lax.axis_index("grp")
@@ -117,7 +117,17 @@
         pl.semaphore_signal(barrier, inc=1, device_id=(lax.rem(g + k, 8), t), device_id_type=MESH)
         return c
 
+    around = (
+        tz * 4 + m4(tx + 1), tz * 4 + m4(tx - 1), m4(tz + 1) * 4 + tx, m4(tz - 1) * 4 + tx,
+    )
+
+    def greet_a(k, c):
+        for a in around:
+            pl.semaphore_signal(barrier, inc=1, device_id=(lax.rem(g + k, 8), a), device_id_type=MESH)
+        return c
+
     lax.fori_loop(1, 16, greet_t, 0)
+    lax.fori_loop(1, 8, greet_a, 0)
     lax.fori_loop(1, 8, greet_g, 0)
 
     step = kv.shape[0] // PARTS
@@ -151,26 +161,19 @@
         here = jnp.clip(lens - 16 * j, 0, 16)
         count = count + jnp.where(page_ids == pt_ref[j : j + 1, :], here, 0)
     live[...] = count.astype(F32).astype(BF16)
-    small[4].wait()
-    pl_m, b0, b1, sign = route_maps(routes_ref[...])
-    place[...] = pl_m
-    back[0] = b0
-    back[1] = b1
     small[2].wait()
     small[3].wait()
     attn = attend(q_ref[...], own_ref[...], live, kv, kv_copies, step)
-    for c in small[5:]:
-        c.wait()
-    ginv[...] = 1.0 / gain_ref[...]
-
-    pl.semaphore_wait(barrier, 22)
+    small[8].wait()
+
+    pl.semaphore_wait(barrier, 50)
 
     def rcopy(src, dst, ss, rr, dev):
         return pltpu.make_async_remote_copy(
             src_ref=src, dst_ref=dst, send_sem=ss, recv_sem=rr, device_id=dev, device_id_type=MESH
         )
 
-    def reduce_scatter(rows, src, rb, y, rc, ss, rr, produce, finish):
+    def reduce_scatter(rows, src, rb, y, rc, ss, rr, produce, last):
         def q_rows(h, q):
             return pl.ds((2 * h + q) * rows, rows)
 
@@ -199,6 +202,16 @@
         def go(m):
             m.start()
             sent.append(m)
+
+        def rows_of(ref, h, q):
+            return lambda c: ref.at[pl.ds((2 * h + q) * rows + c * 64, 64)]
+
+        def halves(ref):
+            return lambda c: ref.at[pl.ds(c * 64, 64)]
+
+        def end(h, q, term, part_of, axis, d):
+            for c in (0, 1):
+                go(last(h, q, c, term, part_of(c), nbr(h, axis, d)[1]))
 
         def stage_g(i):
             produce(i, blk, 0)
@@ -207,8 +220,12 @@
                 go(msg1(h, i, 1))
             produce(i, blk, 1)
             for h in (0, 1):
-                go(msg1(h, i, 2))
-                go(msg1(h, i, 3))
+                if i < 3:
+                    go(msg1(h, i, 2))
+                    go(msg1(h, i, 3))
+                else:
+                    end(h, 1, 1, rows_of(src.at[blk(h, 3, 1)], h, 1), 1, 1)
+                    end(h, 0, 2, rows_of(src.at[blk(h, 3, -1)], h, 0), 1, -1)
 
         def stage_h(i):
             for h in (0, 1):
@@ -216,12 +233,18 @@
                 rb[h, i, 0] = (
                     rb[h, i, 0].astype(F32) + src[blk(h, i, 1), q_rows(h, 0)].astype(F32)
                 ).astype(BF16)
-                go(msg1(h, i, 4, 0))
+                if i < 3:
+                    go(msg1(h, i, 4, 0))
+                else:
+                    end(h, 0, 1, halves(rb.at[h, i, 0]), 1, 1)
                 msg1(h, i, 1).wait_recv()
                 rb[h, i, 1] = (
                     rb[h, i, 1].astype(F32) + src[blk(h, i, -1), q_rows(h, 1)].astype(F32)
                 ).astype(BF16)
-                go(msg1(h, i, 5, 1))
+                if i < 3:
+                    go(msg1(h, i, 5, 1))
+                else:
+                    end(h, 1, 2, halves(rb.at[h, i, 1]), 1, -1)
 
         def stage_j(i):
             produce(i, blk, 2)
@@ -237,15 +260,15 @@
                     if i == 0:
                         go(msg2(h, q, 0))
                 if i == 1:
-                    go(msg2(h, 2, 1))
+                    end(h, 1, 3, lambda c: y.at[h, 1, pl.ds(rows + c * 64, 64)], 0, 1)
                     msg2(h, 0, 1).wait_recv()
                     rc[h, 0] = (rc[h, 0].astype(F32) + y[h, 1, pl.ds(0, rows)].astype(F32)).astype(BF16)
-                    go(msg2(h, 4, 1, 0))
+                    end(h, 0, 3, halves(rc.at[h, 0]), 0, 1)
                 if i == 2:
-                    go(msg2(h, 3, 2))
+                    end(h, 0, 4, lambda c: y.at[h, 2, pl.ds(c * 64, 64)], 0, -1)
                     msg2(h, 1, 2).wait_recv()
                     rc[h, 1] = (rc[h, 1].astype(F32) + y[h, 2, pl.ds(rows, rows)].astype(F32)).astype(BF16)
-                    go(msg2(h, 5, 2, 1))
+                    end(h, 1, 4, halves(rc.at[h, 1]), 0, -1)
 
         stage_g(0)
         stage_g(1)
@@ -254,22 +277,12 @@
         stage_h(1)
         stage_j(0)
         stage_g(3)
+        produce(3, blk, 2)
+        own_terms(sent)
         stage_h(2)
         stage_j(1)
         stage_h(3)
         stage_j(2)
-        stage_j(3)
-        for h in (0, 1):
-            for q, (k1, k2) in ((0, (3, 4)), (1, (2, 5))):
-                msg2(h, k1, 3).wait_recv()
-                msg2(h, k2, 3).wait_recv()
-                finish(
-                    h,
-                    q,
-                    y[h, 3, pl.ds(q * rows, rows)].astype(F32)
-                    + rc[h, k1].astype(F32)
-                    + rc[h, k2].astype(F32),
-                )
         return sent
 
     sent1 = []
@@ -317,6 +330,14 @@
         for k in range(3):
             for h in (0, 1):
                 go1(out1(h, i, k))
+    small[4].wait()
+    pl_m, b0, b1, sign = route_maps(routes_ref[...])
+    place[...] = pl_m
+    back[0] = b0
+    back[1] = b1
+    for c in small[5:8]:
+        c.wait()
+    ginv[...] = 1.0 / gain_ref[...]
     gain_row = gain_ref[:, pl.ds(pl.multiple_of(t * CW, 128), CW)]
     for i in range(4):
         for h in (0, 1):
@@ -548,37 +569,40 @@
                     hv, wd[:, pl.ds(pl.multiple_of(b * CW, 128), CW)], preferred_element_type=F32
                 ).astype(BF16)
 
-    def back_copy(slot):
-        p = slot // 2
-        r = lax.rem(p, 2) * 2 + p // 2
-        dst = lax.rem(gy + r, 4) * 2 + lax.rem(slot, 2)
+    def home(h, q, c):
+        r = (0, 2, 1, 3)[2 * h + q]
+        return lax.rem(gy + r, 4) * 2 + c
+
+    def last(h, q, c, term, src, to):
+        n = ((2 * h + q) * 2 + c) * 5 + term
         return rcopy(
-            fin.at[pl.ds(pl.multiple_of(slot * 64, 64), 64)],
-            ret.at[pl.ds(pl.multiple_of(g * 64, 64), 64)],
-            rt_s.at[slot],
-            rt_r.at[g],
-            (dst, t),
+            src, ret.at[term, pl.ds(pl.multiple_of(g * 64, 64), 64)],
+            rt_s.at[n], rt_r.at[term * 8 + g], (home(h, q, c), to),
         )
 
-    def finish2(h, q, v):
-        p = 2 * h + q
-        fin[p * 128 : (p + 1) * 128, :] = v.astype(BF16)
-        for c in (0, 1):
-            slot = p * 2 + c
-            if p == 0:
-
-                @pl.when(gc != c)
-                def _():
-                    back_copy(slot).start()
-
-                @pl.when(gc == c)
-                def _():
-                    ret[pl.ds(pl.multiple_of(g * 64, 64), 64), :] = fin[slot * 64 : slot * 64 + 64, :]
-
-            else:
-                back_copy(slot).start()
-
-    sent2 = reduce_scatter(128, p2, rb2, y2, rc2, a2s, a2r, produce, finish2)
+    def own_term(h, q, c):
+        return last(h, q, c, 0, p2.at[t, pl.ds((2 * h + q) * 128 + c * 64, 64)], t)
+
+    def own_terms(sent):
+        for h in (0, 1):
+            for q in (0, 1):
+                for c in (0, 1):
+                    if h == 0 and q == 0:
+
+                        @pl.when(gc != c)
+                        def _():
+                            own_term(0, 0, c).start()
+
+                        @pl.when(gc == c)
+                        def _():
+                            ret[0, pl.ds(pl.multiple_of(g * 64, 64), 64), :] = p2[t, c * 64 : c * 64 + 64, :]
+
+                    else:
+                        m = own_term(h, q, c)
+                        m.start()
+                        sent.append(m)
+
+    sent2 = reduce_scatter(128, p2, rb2, y2, rc2, a2s, a2r, produce, last)
 
     def stat_wait(k, c):
         stat(k).wait_recv()
@@ -591,14 +615,25 @@
     wa = 1.0 / (1.0 + jnp.exp(-dcol))
     wb = 1.0 / (1.0 + jnp.exp(dcol))
 
+    def term_wait(term, e):
+        at = ret.at[term, pl.ds(pl.multiple_of(e * 64, 64), 64)]
+        rcopy(at, at, rt_s.at[0], rt_r.at[term * 8 + e], (g, t)).wait_recv()
+
     def ret_wait(k, c):
-        e = lax.rem(g + k, 8)
-        at = ret.at[pl.ds(pl.multiple_of(e * 64, 64), 64)]
-        rcopy(at, at, rt_s.at[0], rt_r.at[e], (g, t)).wait_recv()
+        term_wait(0, lax.rem(g + k, 8))
+        return c
+
+    def rest_wait(e, c):
+        for term in (3, 1, 2, 4):
+            term_wait(term, e)
         return c
 
     lax.fori_loop(1, 8, ret_wait, 0)
-    rv = ret[...]
+    lax.fori_loop(0, 8, rest_wait, 0)
+    rv = ret[0].astype(F32)
+    for term in (1, 2, 3, 4):
+        rv = rv + ret[term].astype(F32)
+    rv = rv.astype(BF16)
     out_ref[...] = (
         rs[...].astype(F32)
         + wa * jnp.dot(back[0], rv, preferred_element_type=F32)
@@ -618,15 +653,11 @@
 
     lax.fori_loop(1, 16, stat_sent, 0)
     lax.fori_loop(1, 8, deal_sent, 0)
-    for slot in range(8):
-        if slot < 2:
-
-            @pl.when(gc != slot)
-            def _():
-                back_copy(slot).wait_send()
-
-        else:
-            back_copy(slot).wait_send()
+    for c in (0, 1):
+
+        @pl.when(gc != c)
+        def _():
+            own_term(0, 0, c).wait_send()
 
 
 def local(
@@ -672,8 +703,7 @@
             pltpu.VMEM((128, CW), BF16),
             pltpu.VMEM((128, CW), BF16),
             pltpu.VMEM((8, 64, CW), BF16),
-            pltpu.VMEM((512, CW), BF16),
-            pltpu.VMEM((512, CW), BF16),
+            pltpu.VMEM((5, 512, CW), BF16),
             pltpu.VMEM((8, 128), F32),
             pltpu.VMEM((16, 8, 128), F32),
             pltpu.VMEM((512, 128), BF16),
@@ -689,8 +719,8 @@
             dma((60,)),
             dma((8,)),
             dma((8,)),
-            dma((8,)),
-            dma((8,)),
+            dma((40,)),
+            dma((40,)),
             dma((16,)),
             dma((16,)),
         ],

time: 115 us -> 117 us (1.017)
  Pallas kernels: 113 us -> 115 us
    pallas_call x1, Pallas kernels: 113 us -> 115 us  [local(): pl.pallas_call(layer_kernel, out_shape=jax.ShapeDtypeStruct((128, CW), BF...]
where the time goes in v3:
time: 117 us
  Pallas kernels  115 us (98%)
  local copies, waits for them, and re-layouts  1.54 us (1%)
    pallas_call x1, Pallas kernels, local(): pl.pallas_call(layer_kernel, out_shape=jax.ShapeDtypeStruct((128, CW), BF...  115 us

profile of v3, /device:TPU:1, one launch (start us, length us, event | category | flops | bytes accessed | tf_op | source)
XLA Modules:
  0.0 116.6 jit_solution(10398499759789052818)
XLA Ops:
  0.0 115.0 %layer.1 = bf16[128,384]{1,0:T(8,128)(2,1)} custom-call(bf16[128,256]{1,0:T(8,128)(2,1)} %q_hbm.1, bf16[128,256]{1,0:T(8,128)(2,1)} %bitcast.9, s32[16,128]{1,0:T(8,128)} %bitcast.11, s32[1,128]{1,0:T(1,128)} %bitcast.13, bf16[6400,256]{1,0:T(8,128)(2,1)} %bitcast.7, bf16[256,6144]{1,0:T(8,128)(2,1)} %w_hbm.1, bf16[128,384]{1,0:T(8,128)(2,1)} %res_hbm.1, ...), custom_call_target="tpu_custom_call" | custom-call | flops 11811160064 | bytes 27262976 | tf_op jit(solution)/shard_map/layer/pallas_call | solution.py:670
  115.0 1.5 %copy.15 = bf16[128,384]{1,0:T(8,128)(2,1)} copy(bf16[128,384]{1,0:T(8,128)(2,1)} %layer.1) | data formatting | bytes 196608

commit v4 on v2

--- a/solution.py
+++ b/solution.py
@@ -93,7 +93,7 @@
     q_ref, own_ref, pt_ref, len_ref, kv, w, res_ref, gain_ref, router_ref, routes_ref, live, part, ginv,
     wg, wu, wd, xg, acc, ssq, hid, p2, rb1, y1, rc1, rb2, y2, rc2,
     rs, xs, ds, fin, ret, stat_out, stat_in, place, back,
-    ksem, msem, wsem, a1s, a1r, ags, agr, a2s, a2r, ds_s, ds_r, rt_s, rt_r, st_s, st_r,
+    ksem, msem, wsem, a1s, a1r, ags, agr, a2s, a2r, ds_s, ds_r, ea_s, ea_r, rt_s, rt_r, st_s, st_r,
 ):
     g = lax.axis_index("grp")
     t = lax.axis_index("tp")
@@ -117,6 +117,11 @@
         pl.semaphore_signal(barrier, inc=1, device_id=(lax.rem(g + k, 8), t), device_id_type=MESH)
         return c
 
+    around = (
+        tz * 4 + m4(tx + 1), tz * 4 + m4(tx - 1), m4(tz + 1) * 4 + tx, m4(tz - 1) * 4 + tx,
+    )
+    for a in around:
+        pl.semaphore_signal(barrier, inc=1, device_id=(gy * 2 + 1 - gc, a), device_id_type=MESH)
     lax.fori_loop(1, 16, greet_t, 0)
     lax.fori_loop(1, 8, greet_g, 0)
 
@@ -151,19 +156,12 @@
         here = jnp.clip(lens - 16 * j, 0, 16)
         count = count + jnp.where(page_ids == pt_ref[j : j + 1, :], here, 0)
     live[...] = count.astype(F32).astype(BF16)
-    small[4].wait()
-    pl_m, b0, b1, sign = route_maps(routes_ref[...])
-    place[...] = pl_m
-    back[0] = b0
-    back[1] = b1
     small[2].wait()
     small[3].wait()
     attn = attend(q_ref[...], own_ref[...], live, kv, kv_copies, step)
-    for c in small[5:]:
-        c.wait()
-    ginv[...] = 1.0 / gain_ref[...]
-
-    pl.semaphore_wait(barrier, 22)
+    small[8].wait()
+
+    pl.semaphore_wait(barrier, 26)
 
     def rcopy(src, dst, ss, rr, dev):
         return pltpu.make_async_remote_copy(
@@ -317,6 +315,16 @@
         for k in range(3):
             for h in (0, 1):
                 go1(out1(h, i, k))
+    small[4].wait()
+    pl_m, b0, b1, sign = route_maps(routes_ref[...])
+    place[...] = pl_m
+    back[0] = b0
+    back[1] = b1
+    for c in small[5:8]:
+        c.wait()
+    ginv[...] = 1.0 / gain_ref[...]
+    acc[...] = jnp.zeros_like(acc)
+    ssq[...] = jnp.zeros_like(ssq)
     gain_row = gain_ref[:, pl.ds(pl.multiple_of(t * CW, 128), CW)]
     for i in range(4):
         for h in (0, 1):
@@ -348,6 +356,21 @@
     own_row, own_slot = seat(gy, gc, gy)
     xg[t, pl.ds(own_row, 64), :] = ds[g]
 
+    def early(c, d):
+        return rcopy(
+            ds.at[gy * 2 + c], xg.at[t, pl.ds(pl.multiple_of(gc * 64, 64), 64)],
+            ea_s.at[c * 4 + d], ea_r.at[d * 2 + gc], (gy * 2 + c, around[d]),
+        )
+
+    def early_wait(d):
+        for c in (0, 1):
+            at = xg.at[around[d ^ 1], pl.ds(c * 64, 64)]
+            rcopy(at, at, ea_s.at[0], ea_r.at[d * 2 + c], (g, t)).wait_recv()
+
+    for d in range(4):
+        for c in (0, 1):
+            early(c, d).start()
+
     def deal(k):
         e = lax.rem(g + k, 8)
         row, slot = seat(gy, gc, e // 2)
@@ -411,24 +434,18 @@
         send(h, 1, i, 2 + q, b)
 
     def own_quarter(h, q):
-        p = 2 * h + q
         for c in (0, 1):
-            slot = p * 2 + c
-            if p == 0:
-
-                @pl.when(gc != c)
-                def _():
-                    dealt(slot).wait_recv()
-
-            else:
-                dealt(slot).wait_recv()
+            dealt((2 * h + q) * 2 + c).wait_recv()
         send(h, 0, 0, q, t)
         send(h, 0, 0, 2 + q, t)
 
     def stage_f(i):
         for h in (0, 1):
             b = ab(h, OFFS_OUT[i], -1)
-            wait(h, 1, i, 0, b)
+            if (i, h) == (0, 0):
+                early_wait(2)
+            else:
+                wait(h, 1, i, 0, b)
             send(h, 1, i, 4, b)
             b = ab(h, OFFS_OUT[i], 1)
             wait(h, 1, i, 3, b)
@@ -437,7 +454,10 @@
     def stage_w1(i):
         for h in (0, 1):
             wait(h, 1, i, 1, ab(h, OFFS_OUT[i], -1))
-            wait(h, 1, i, 2, ab(h, OFFS_OUT[i], 1))
+            if (i, h) == (0, 0):
+                early_wait(3)
+            else:
+                wait(h, 1, i, 2, ab(h, OFFS_OUT[i], 1))
 
     def stage_w2(i):
         for h in (0, 1):
@@ -467,24 +487,19 @@
 
         lax.fori_loop(0, len(offsets) * 2, body, 0)
 
-    own_quarter(0, 0)
-    spread(0, 0, 0)
+    lo = [ab(h, -1, 0) for h in (0, 1)]
+    hi = [ab(h, 1, 0) for h in (0, 1)]
     own_quarter(1, 0)
     own_quarter(1, 1)
-    own_quarter(0, 1)
+    early_wait(0)
+    send(0, 0, 0, 4, lo[0])
+    spread(0, 1, 0)
+    early_wait(1)
+    spread(0, 2, 0)
     spread(1, 0, 0)
     spread(1, 0, 1)
+    own_quarter(0, 1)
     spread(0, 0, 1)
-    acc[...] = jnp.zeros_like(acc)
-    ssq[...] = jnp.zeros_like(ssq)
-
-    lo = [ab(h, -1, 0) for h in (0, 1)]
-    hi = [ab(h, 1, 0) for h in (0, 1)]
-    wait(0, 0, 0, 0, lo[0])
-    send(0, 0, 0, 4, lo[0])
-    spread(0, 1, 0)
-    wait(0, 0, 0, 2, hi[0])
-    spread(0, 2, 0)
     wait(1, 0, 0, 0, lo[1])
     send(1, 0, 0, 4, lo[1])
     wait(1, 0, 0, 3, hi[1])
@@ -502,6 +517,7 @@
     spread(1, 2, 0)
     wcopies[0].wait()
     wcopies[1].wait()
+    dealt(1 - gc).wait_recv()
     eat((0, 0))
     stage_f(0)
     for h in (0, 1):
@@ -618,6 +634,9 @@
 
     lax.fori_loop(1, 16, stat_sent, 0)
     lax.fori_loop(1, 8, deal_sent, 0)
+    for d in range(4):
+        for c in (0, 1):
+            early(c, d).wait_send()
     for slot in range(8):
         if slot < 2:
 
@@ -691,6 +710,8 @@
             dma((8,)),
             dma((8,)),
             dma((8,)),
+            dma((8,)),
+            dma((8,)),
             dma((16,)),
             dma((16,)),
         ],

time: 115 us -> 115 us (level)
  no operation moved by 1% of the time
where the time goes in v4:
time: 115 us
  Pallas kernels  113 us (98%)
  local copies, waits for them, and re-layouts  1.54 us (1%)
    pallas_call x1, Pallas kernels, local(): pl.pallas_call(layer_kernel, out_shape=jax.ShapeDtypeStruct((128, CW), BF...  113 us

profile of v4, /device:TPU:1, one launch (start us, length us, event | category | flops | bytes accessed | tf_op | source)
XLA Modules:
  0.0 114.8 jit_solution(8562698499733184841)
XLA Ops:
  0.0 113.3 %layer.1 = bf16[128,384]{1,0:T(8,128)(2,1)} custom-call(bf16[128,256]{1,0:T(8,128)(2,1)} %q_hbm.1, bf16[128,256]{1,0:T(8,128)(2,1)} %bitcast.9, s32[16,128]{1,0:T(8,128)} %bitcast.11, s32[1,128]{1,0:T(1,128)} %bitcast.13, bf16[6400,256]{1,0:T(8,128)(2,1)} %bitcast.7, bf16[256,6144]{1,0:T(8,128)(2,1)} %w_hbm.1, bf16[128,384]{1,0:T(8,128)(2,1)} %res_hbm.1, ...), custom_call_target="tpu_custom_call" | custom-call | flops 11811160064 | bytes 27262976 | tf_op jit(solution)/shard_map/layer/pallas_call | solution.py:658
  113.3 1.5 %copy.15 = bf16[128,384]{1,0:T(8,128)(2,1)} copy(bf16[128,384]{1,0:T(8,128)(2,1)} %layer.1) | data formatting | bytes 196608

commit v5 on v4

--- a/solution.py
+++ b/solution.py
@@ -290,31 +290,149 @@
         c[axis] = m4(c[axis] + o)
         return (g, tid(h, c[0], c[1]))
 
-    def out1(h, i, k):
+    def cols(kc):
+        return pl.ds(kc * 128, 128)
+
+    def out1(h, i, k, kc):
         o1, o2 = OFFS_IN[i], (2, 1, -1)[k]
-        n = h * 12 + i * 3 + k
+        n = kc * 30 + h * 12 + i * 3 + k
         return rcopy(
-            part.at[tid(h, m4(me[h][0] + o1), m4(me[h][1] + o2)), pl.ds(h * 64, 64)],
-            rb1.at[h, i, k], a1s.at[n], a1r.at[n], far(h, 1, o2),
-        )
-
-    def out2(h, i):
-        n = 24 + h * 3 + i
-        return rcopy(y1.at[h, i], rc1.at[h, i], a1s.at[n], a1r.at[n], far(h, 0, OFFS_IN[i]))
+            part.at[tid(h, m4(me[h][0] + o1), m4(me[h][1] + o2)), pl.ds(h * 64, 64), cols(kc)],
+            rb1.at[h, i, k, :, cols(kc)], a1s.at[n], a1r.at[n], far(h, 1, o2),
+        )
+
+    def out2(h, i, kc):
+        n = kc * 30 + 24 + h * 3 + i
+        return rcopy(
+            y1.at[h, i, :, cols(kc)], rc1.at[h, i, :, cols(kc)], a1s.at[n], a1r.at[n], far(h, 0, OFFS_IN[i])
+        )
 
     def go1(m):
         m.start()
         sent1.append(m)
 
+    def first_step(kc, groups):
+        for i in groups:
+            for k in range(3):
+                for h in (0, 1):
+                    go1(out1(h, i, k, kc))
+
+    def term1(h, i, kc):
+        for k in range(3):
+            out1(h, i, k, kc).wait_recv()
+        v = part[tid(h, m4(me[h][0] + OFFS_IN[i]), me[h][1]), h * 64 : h * 64 + 64, cols(kc)].astype(F32)
+        for k in range(3):
+            v = v + rb1[h, i, k, :, cols(kc)].astype(F32)
+        return v
+
+    def second_step(kc):
+        for i in range(3):
+            for h in (0, 1):
+                y1[h, i, :, cols(kc)] = term1(h, i, kc).astype(BF16)
+                go1(out2(h, i, kc))
+
+    def finish1(kc):
+        gain_row = gain_ref[:, pl.ds(pl.multiple_of(t * CW + kc * 128, 128), 128)]
+        for h in (0, 1):
+            v = term1(h, 3, kc)
+            for k in range(3):
+                out2(h, k, kc).wait_recv()
+                v = v + rc1[h, k, :, cols(kc)].astype(F32)
+            at = pl.ds(h * 64, 64)
+            r = (res_ref[at, cols(kc)].astype(F32) + v).astype(BF16)
+            rs[at, cols(kc)] = r
+            xs[at, cols(kc)] = (r.astype(F32) * gain_row).astype(BF16)
+
+    def seat(src_y, src_c, dst_y):
+        r = m4(src_y - dst_y)
+        p = lax.rem(r, 2) * 2 + r // 2
+        return pl.multiple_of(p * 128 + src_c * 64, 64), p * 2 + src_c
+
+    own_row, own_slot = seat(gy, gc, gy)
+
+    def early(c, d, kc):
+        return rcopy(
+            ds.at[gy * 2 + c, :, cols(kc)], xg.at[t, pl.ds(pl.multiple_of(gc * 64, 64), 64), cols(kc)],
+            ea_s.at[kc * 8 + c * 4 + d], ea_r.at[kc * 8 + d * 2 + gc], (gy * 2 + c, around[d]),
+        )
+
+    def early_wait(d):
+        for c in (0, 1):
+            for kc in range(3):
+                at = xg.at[around[d ^ 1], pl.ds(c * 64, 64), cols(kc)]
+                rcopy(at, at, ea_s.at[0], ea_r.at[kc * 8 + d * 2 + c], (g, t)).wait_recv()
+
+    def deal(k, kc):
+        e = lax.rem(g + k, 8)
+        row, slot = seat(gy, gc, e // 2)
+        return rcopy(
+            ds.at[e, :, cols(kc)], xg.at[t, pl.ds(row, 64), cols(kc)],
+            ds_s.at[kc * 8 + k], ds_r.at[kc * 8 + slot], (e, t),
+        )
+
+    def dealt(slot, kc):
+        at = xg.at[t, pl.ds(pl.multiple_of(slot * 64, 64), 64), cols(kc)]
+        return rcopy(at, at, ds_s.at[0], ds_r.at[kc * 8 + slot], (g, t))
+
+    def deal_out(kc):
+        ds[:, :, cols(kc)] = (
+            jnp.dot(place[...], xs[:, cols(kc)], preferred_element_type=F32).astype(BF16).reshape(8, 64, 128)
+        )
+        xg[t, pl.ds(own_row, 64), cols(kc)] = ds[g, :, cols(kc)]
+        for d in range(4):
+            for c in (0, 1):
+                early(c, d, kc).start()
+
+        def deal_start(k, c):
+            deal(k, kc).start()
+            return c
+
+        lax.fori_loop(1, 8, deal_start, 0)
+
+    ag_sent = []
+
+    def ag(h, phase, i, k, b, kc=None):
+        q, d = ((0, 1), (1, 1), (0, -1), (1, -1), (0, 1), (1, -1))[k]
+        c = list(me[h])
+        c[phase] = m4(c[phase] + d)
+        rows = pl.ds((2 * h + q) * 128, 128)
+        ref = xg.at[b, rows] if kc is None else xg.at[b, rows, cols(kc)]
+        n = h * 30 + phase * 6 + i * 6 + k + (0 if kc is None else 60 * kc)
+        return rcopy(ref, ref, ags.at[n], agr.at[n], (g, tid(h, c[0], c[1])))
+
+    def send(*a):
+        m = ag(*a)
+        m.start()
+        ag_sent.append(m)
+
+    def ab(h, o1, o2):
+        return tid(h, m4(me[h][0] + o1), m4(me[h][1] + o2))
+
+    def wait(h, phase, i, k, b):
+        if k < 4 and i == 0:
+            for kc in range(3):
+                ag(h, phase, i, k, b, kc).wait_recv()
+        else:
+            ag(h, phase, i, k, b).wait_recv()
+
+    def spread(h, i, q):
+        b = ab(h, OFFS_OUT[i], 0)
+        send(h, 1, i, q, b)
+        send(h, 1, i, 2 + q, b)
+
+    def own_sends(kc):
+        for h, q in ((1, 0), (1, 1), (0, 1)):
+            for c in (0, 1):
+                dealt((2 * h + q) * 2 + c, kc).wait_recv()
+            for phase in (0, 1):
+                for k in (q, 2 + q):
+                    send(h, phase, 0, k, t, kc)
+
     lax.fori_loop(0, 7, project, 0)
-    for k in range(3):
-        for h in (0, 1):
-            go1(out1(h, 0, k))
+    first_step(0, (0,))
     lax.fori_loop(7, 16, project, 0)
-    for i in (1, 2, 3):
-        for k in range(3):
-            for h in (0, 1):
-                go1(out1(h, i, k))
+    first_step(0, (1, 2, 3))
+    first_step(1, (0, 1, 2, 3))
     small[4].wait()
     pl_m, b0, b1, sign = route_maps(routes_ref[...])
     place[...] = pl_m
@@ -322,69 +440,19 @@
     back[1] = b1
     for c in small[5:8]:
         c.wait()
-    ginv[...] = 1.0 / gain_ref[...]
-    acc[...] = jnp.zeros_like(acc)
-    ssq[...] = jnp.zeros_like(ssq)
-    gain_row = gain_ref[:, pl.ds(pl.multiple_of(t * CW, 128), CW)]
-    for i in range(4):
-        for h in (0, 1):
-            for k in range(3):
-                out1(h, i, k).wait_recv()
-            v = part[tid(h, m4(me[h][0] + OFFS_IN[i]), me[h][1]), h * 64 : h * 64 + 64, :].astype(F32)
-            for k in range(3):
-                v = v + rb1[h, i, k].astype(F32)
-            if i < 3:
-                y1[h, i] = v.astype(BF16)
-                go1(out2(h, i))
-            else:
-                for k in range(3):
-                    out2(h, k).wait_recv()
-                    v = v + rc1[h, k].astype(F32)
-                at = pl.ds(h * 64, 64)
-                r = (res_ref[at, :].astype(F32) + v).astype(BF16)
-                rs[at, :] = r
-                xs[at, :] = (r.astype(F32) * gain_row).astype(BF16)
-
+    second_step(0)
+    first_step(2, (0, 1, 2, 3))
+    second_step(1)
+    finish1(0)
+    deal_out(0)
+    second_step(2)
+    finish1(1)
+    deal_out(1)
+    own_sends(0)
+    finish1(2)
+    deal_out(2)
+    own_sends(1)
     x = xs[...]
-    ds[...] = jnp.dot(place[...], x, preferred_element_type=F32).astype(BF16).reshape(8, 64, CW)
-
-    def seat(src_y, src_c, dst_y):
-        r = m4(src_y - dst_y)
-        p = lax.rem(r, 2) * 2 + r // 2
-        return pl.multiple_of(p * 128 + src_c * 64, 64), p * 2 + src_c
-
-    own_row, own_slot = seat(gy, gc, gy)
-    xg[t, pl.ds(own_row, 64), :] = ds[g]
-
-    def early(c, d):
-        return rcopy(
-            ds.at[gy * 2 + c], xg.at[t, pl.ds(pl.multiple_of(gc * 64, 64), 64)],
-            ea_s.at[c * 4 + d], ea_r.at[d * 2 + gc], (gy * 2 + c, around[d]),
-        )
-
-    def early_wait(d):
-        for c in (0, 1):
-            at = xg.at[around[d ^ 1], pl.ds(c * 64, 64)]
-            rcopy(at, at, ea_s.at[0], ea_r.at[d * 2 + c], (g, t)).wait_recv()
-
-    for d in range(4):
-        for c in (0, 1):
-            early(c, d).start()
-
-    def deal(k):
-        e = lax.rem(g + k, 8)
-        row, slot = seat(gy, gc, e // 2)
-        return rcopy(ds.at[e], xg.at[t, pl.ds(row, 64)], ds_s.at[k], ds_r.at[slot], (e, t))
-
-    def deal_start(k, c):
-        deal(k).start()
-        return c
-
-    lax.fori_loop(1, 8, deal_start, 0)
-
-    def dealt(slot):
-        at = xg.at[t, pl.ds(pl.multiple_of(slot * 64, 64), 64)]
-        return rcopy(at, at, ds_s.at[0], ds_r.at[slot], (g, t))
 
     logit = lax.dot_general(
         router_ref[:, pl.ds(pl.multiple_of(t * CW, 128), CW)], x, NT, preferred_element_type=F32
@@ -406,38 +474,6 @@
         return c
 
     lax.fori_loop(1, 16, stat_start, 0)
-
-    ag_sent = []
-
-    def ag(h, phase, i, k, b):
-        q, d = ((0, 1), (1, 1), (0, -1), (1, -1), (0, 1), (1, -1))[k]
-        c = list(me[h])
-        c[phase] = m4(c[phase] + d)
-        ref = xg.at[b, pl.ds((2 * h + q) * 128, 128)]
-        n = h * 30 + phase * 6 + i * 6 + k
-        return rcopy(ref, ref, ags.at[n], agr.at[n], (g, tid(h, c[0], c[1])))
-
-    def send(*a):
-        m = ag(*a)
-        m.start()
-        ag_sent.append(m)
-
-    def ab(h, o1, o2):
-        return tid(h, m4(me[h][0] + o1), m4(me[h][1] + o2))
-
-    def wait(h, phase, i, k, b):
-        ag(h, phase, i, k, b).wait_recv()
-
-    def spread(h, i, q):
-        b = ab(h, OFFS_OUT[i], 0)
-        send(h, 1, i, q, b)
-        send(h, 1, i, 2 + q, b)
-
-    def own_quarter(h, q):
-        for c in (0, 1):
-            dealt((2 * h + q) * 2 + c).wait_recv()
-        send(h, 0, 0, q, t)
-        send(h, 0, 0, 2 + q, t)
 
     def stage_f(i):
         for h in (0, 1):
@@ -489,17 +525,15 @@
 
     lo = [ab(h, -1, 0) for h in (0, 1)]
     hi = [ab(h, 1, 0) for h in (0, 1)]
-    own_quarter(1, 0)
-    own_quarter(1, 1)
+    own_sends(2)
+    ginv[...] = 1.0 / gain_ref[...]
+    acc[...] = jnp.zeros_like(acc)
+    ssq[...] = jnp.zeros_like(ssq)
     early_wait(0)
     send(0, 0, 0, 4, lo[0])
     spread(0, 1, 0)
     early_wait(1)
     spread(0, 2, 0)
-    spread(1, 0, 0)
-    spread(1, 0, 1)
-    own_quarter(0, 1)
-    spread(0, 0, 1)
     wait(1, 0, 0, 0, lo[1])
     send(1, 0, 0, 4, lo[1])
     wait(1, 0, 0, 3, hi[1])
@@ -517,7 +551,8 @@
     spread(1, 2, 0)
     wcopies[0].wait()
     wcopies[1].wait()
-    dealt(1 - gc).wait_recv()
+    for kc in range(3):
+        dealt(1 - gc, kc).wait_recv()
     eat((0, 0))
     stage_f(0)
     for h in (0, 1):
@@ -629,14 +664,16 @@
         return c
 
     def deal_sent(k, c):
-        deal(k).wait_send()
+        for kc in range(3):
+            deal(k, kc).wait_send()
         return c
 
     lax.fori_loop(1, 16, stat_sent, 0)
     lax.fori_loop(1, 8, deal_sent, 0)
     for d in range(4):
         for c in (0, 1):
-            early(c, d).wait_send()
+            for kc in range(3):
+                early(c, d, kc).wait_send()
     for slot in range(8):
         if slot < 2:
 
@@ -700,16 +737,16 @@
             dma((PARTS,)),
             dma((9,)),
             dma((3,)),
-            dma((30,)),
-            dma((30,)),
+            dma((90,)),
+            dma((90,)),
+            dma((180,)),
+            dma((180,)),
             dma((60,)),
             dma((60,)),
-            dma((60,)),
-            dma((60,)),
-            dma((8,)),
-            dma((8,)),
-            dma((8,)),
-            dma((8,)),
+            dma((24,)),
+            dma((24,)),
+            dma((24,)),
+            dma((24,)),
             dma((8,)),
             dma((8,)),
             dma((16,)),

time: 115 us -> 116 us (level)
  Pallas kernels: 113 us -> 115 us
    pallas_call x1, Pallas kernels: 113 us -> 115 us  [local(): pl.pallas_call(layer_kernel, out_shape=jax.ShapeDtypeStruct((128, CW), BF...]
where the time goes in v5:
time: 116 us
  Pallas kernels  115 us (99%)
  local copies, waits for them, and re-layouts  1.54 us (1%)
    pallas_call x1, Pallas kernels, local(): pl.pallas_call(layer_kernel, out_shape=jax.ShapeDtypeStruct((128, CW), BF...  115 us

profile of v5, /device:TPU:1, one launch (start us, length us, event | category | flops | bytes accessed | tf_op | source)
XLA Modules:
  0.0 116.3 jit_solution(5800692928487131556)
XLA Ops:
  0.0 114.7 %layer.1 = bf16[128,384]{1,0:T(8,128)(2,1)} custom-call(bf16[128,256]{1,0:T(8,128)(2,1)} %q_hbm.1, bf16[128,256]{1,0:T(8,128)(2,1)} %bitcast.9, s32[16,128]{1,0:T(8,128)} %bitcast.11, s32[1,128]{1,0:T(1,128)} %bitcast.13, bf16[6400,256]{1,0:T(8,128)(2,1)} %bitcast.7, bf16[256,6144]{1,0:T(8,128)(2,1)} %w_hbm.1, bf16[128,384]{1,0:T(8,128)(2,1)} %res_hbm.1, ...), custom_call_target="tpu_custom_call" | custom-call | flops 11811160064 | bytes 27262976 | tf_op jit(solution)/shard_map/layer/pallas_call | solution.py:695
  114.7 1.5 %copy.15 = bf16[128,384]{1,0:T(8,128)(2,1)} copy(bf16[128,384]{1,0:T(8,128)(2,1)} %layer.1) | data formatting | bytes 196608
